TPU v7x, 32 devices: a whole 2x2x4 slice. The times are simulated.
32 devices in a mesh: dp: 4 (over y, core), expert: 2 (over x), seq: 4 (over z).
Axes of the slice: x: 2, y: 2, z: 4, core: 2. Of those that a mesh axis runs over, the one named last changes fastest.
Arguments:
- tokens: bfloat16 [16, 1024, 768], P(('dp', 'expert'), 'seq'), may hold values from -6 to 6
- attn_gain: float32 [768], replicated, may hold values from 0.5 to 1.5
- w_query: bfloat16 [768, 768], P(('dp', 'expert')), may hold values from -0.21875 to 0.21875
- w_key: bfloat16 [768, 768], P(('dp', 'expert')), may hold values from -0.21875 to 0.21875
- w_value: bfloat16 [768, 768], P(('dp', 'expert')), may hold values from -0.21875 to 0.21875
- output_projection_weight: bfloat16 [768, 768], P(('dp', 'expert')), may hold values from -3.5 to 3.5
- bias_table: float32 [32, 12], replicated, may hold values from -5 to 5
- rel_buckets: int32 [2047], replicated, may hold values from 0 to 31
- ffn_gain: float32 [768], replicated, may hold values from 0.5 to 1.5
- router: bfloat16 [768, 2], replicated, may hold values from -0.15625 to 0.15625
- expert_in: bfloat16 [2, 768, 3072], P('expert', 'dp'), may hold values from -0.21875 to 0.21875
- expert_out: bfloat16 [2, 3072, 768], P('expert', 'dp'), may hold values from -0.375 to 0.375
- expert_ids: int32 [16, 1024], P(('dp', 'expert'), 'seq'), may hold values from 0 to 1
- cotangent: bfloat16 [16, 1024, 768], P(('dp', 'expert'), 'seq'), may hold values from -6 to 6
Outputs:
- layer_out: bfloat16 [16, 1024, 768], P(('dp', 'expert'), 'seq')
- input_grad: float32 [16, 1024, 768], P(('dp', 'expert'), 'seq')
- attn_gain_grad: float32 [768], replicated
- query_grad: float32 [768, 768], P(('dp', 'expert'))
- key_grad: float32 [768, 768], P(('dp', 'expert'))
- value_grad: float32 [768, 768], P(('dp', 'expert'))
- output_grad: float32 [768, 768], P(('dp', 'expert'))
- table_grad: float32 [32, 12], replicated
- ffn_gain_grad: float32 [768], replicated
- router_grad: float32 [768, 2], replicated
- expert_in_grad: float32 [2, 768, 3072], P('expert', 'dp')
- expert_out_grad: float32 [2, 3072, 768], P('expert', 'dp')
All inputs are finite; a program needn't handle non-finite values.
Results may differ from a plain program's by a relative error of at most 0.018.
Values may be sent and summed in bfloat16 or wider, within the bound.
A program may use at most 192 MiB of HBM per device.

v0:
```python
import math

import jax
import jax.numpy as jnp
from jax import lax
from jax.sharding import PartitionSpec as P

eps = 1e-06
highest_precision = lax.Precision.HIGHEST


def activation(values):
    return jax.nn.gelu(values, approximate=False)


def normalize(residual_stream, gain):
    factor = lax.rsqrt(jnp.mean(residual_stream * residual_stream, axis=-1, keepdims=True) + eps)
    return (residual_stream * factor * gain, factor)


def norm_back(grad_norm, residual_stream, factor, gain):
    gain_grad = jnp.sum(grad_norm * residual_stream * factor, axis=0)
    scaled = grad_norm * gain
    inner = jnp.mean(scaled * residual_stream, axis=-1, keepdims=True)
    return (scaled * factor - residual_stream * factor**3 * inner, gain_grad)


def skew_bias(rel_heads, start, block, length):
    span = length + block - 1
    head_count = rel_heads.shape[0]
    values = lax.dynamic_slice_in_dim(rel_heads, length - block - start, span, 1)
    tiled = jnp.broadcast_to(values[:, None, :], (head_count, block, span)).reshape(
        head_count, block * span
    )
    tiled = jnp.pad(tiled, ((0, 0), (0, block)))
    shaped = tiled.reshape(head_count, block, span + 1)[:, :, :length]
    return jnp.flip(shaped, axis=1)


def diagonal_sums(values, block, length):
    head_count = values.shape[0]
    span = length + block - 1
    flipped = jnp.flip(values, axis=1)
    padded = jnp.pad(flipped, ((0, 0), (0, 0), (0, block)))
    flat = padded.reshape(head_count, block * (length + block))[:, : block * span]
    return jnp.sum(flat.reshape(head_count, block, span), axis=1)


def expert_shards(first_grad, second_grad):
    return (
        lax.psum_scatter(
            first_grad.astype(jnp.bfloat16), "dp", scatter_dimension=1, tiled=True
        ).astype(jnp.float32),
        lax.psum_scatter(
            second_grad.astype(jnp.bfloat16), "dp", scatter_dimension=1, tiled=True
        ).astype(jnp.float32),
    )


def across_replicas(first_grad, second_grad, query_part, key_part, value_part, output_part):
    return (
        lax.psum(first_grad.astype(jnp.bfloat16), "seq").astype(jnp.float32),
        lax.psum(second_grad.astype(jnp.bfloat16), "seq").astype(jnp.float32),
        lax.psum(query_part.astype(jnp.bfloat16), "seq").astype(jnp.float32),
        lax.psum(key_part.astype(jnp.bfloat16), "seq").astype(jnp.float32),
        lax.psum(value_part.astype(jnp.bfloat16), "seq").astype(jnp.float32),
        lax.psum(output_part.astype(jnp.bfloat16), "seq").astype(jnp.float32),
    )


def local(
    tokens,
    attn_gain,
    w_query,
    w_key,
    w_value,
    output_projection_weight,
    bias_table,
    rel_buckets,
    ffn_gain,
    router,
    expert_in,
    expert_out,
    expert_ids,
    cotangent,
):
    seq_count, piece, width = tokens.shape
    groups = lax.axis_size("seq")
    length = piece * groups
    rows = seq_count * piece
    bucket_count, heads_all = bias_table.shape
    local_heads = heads_all // groups
    head_width = width // heads_all
    group_width = local_heads * head_width
    experts = router.shape[1]
    capacity = (5 * rows + 4 * experts - 1) // (4 * experts)
    block = min(512, length)
    block_count = length // block
    factor_scale = 1.0 / math.sqrt(head_width)
    full_query, full_key, full_value, full_output = (
        lax.all_gather(w_query, ("dp", "expert"), axis=0, tiled=True),
        lax.all_gather(w_key, ("dp", "expert"), axis=0, tiled=True),
        lax.all_gather(w_value, ("dp", "expert"), axis=0, tiled=True),
        lax.all_gather(output_projection_weight, ("dp", "expert"), axis=0, tiled=True),
    )
    first_full, second_full = (
        lax.all_gather(expert_in, "dp", axis=1, tiled=True),
        lax.all_gather(expert_out, "dp", axis=1, tiled=True),
    )
    first_weight = first_full[0]
    second_weight = second_full[0]
    residual_stream = tokens.reshape(rows, width).astype(jnp.float32)
    normed_one, factor_one = normalize(residual_stream, attn_gain)
    first_layer_norm = normed_one.astype(jnp.bfloat16)
    query_rows = jnp.dot(first_layer_norm, full_query, preferred_element_type=jnp.float32).astype(
        jnp.bfloat16
    )
    key_rows = jnp.dot(first_layer_norm, full_key, preferred_element_type=jnp.float32).astype(
        jnp.bfloat16
    )
    value_rows = jnp.dot(first_layer_norm, full_value, preferred_element_type=jnp.float32).astype(
        jnp.bfloat16
    )

    def to_groups(values):
        return values.reshape(seq_count, piece, groups, group_width)

    heads_query, heads_key, heads_value = (
        lax.all_to_all(to_groups(query_rows), "seq", split_axis=2, concat_axis=1, tiled=True),
        lax.all_to_all(to_groups(key_rows), "seq", split_axis=2, concat_axis=1, tiled=True),
        lax.all_to_all(to_groups(value_rows), "seq", split_axis=2, concat_axis=1, tiled=True),
    )
    heads_query = heads_query.reshape(seq_count, length, local_heads, head_width)
    heads_key = heads_key.reshape(seq_count, length, local_heads, head_width)
    heads_value = heads_value.reshape(seq_count, length, local_heads, head_width)
    head_start = lax.axis_index("seq") * local_heads
    table_part = lax.dynamic_slice_in_dim(bias_table, head_start, local_heads, 1)
    bucket_onehot = (rel_buckets[:, None] == jnp.arange(bucket_count)[None, :]).astype(jnp.float32)
    rel_heads = jnp.dot(table_part.T, bucket_onehot.T, precision=highest_precision)
    starts = jnp.arange(block_count) * block

    def attend_block(query_block, key_seq, value_seq, start):
        bias = skew_bias(rel_heads, start, block, length)
        scores = (
            jnp.einsum("qhd,khd->hqk", query_block, key_seq, preferred_element_type=jnp.float32)
            * factor_scale
            + bias
        )
        peak = jnp.max(scores, axis=-1, keepdims=True)
        weights = jnp.exp(scores - peak)
        totals = jnp.sum(weights, axis=-1, keepdims=True)
        rounded = (weights / totals).astype(jnp.bfloat16)
        mixed = jnp.einsum("hqk,khd->qhd", rounded, value_seq, preferred_element_type=jnp.float32)
        return (mixed.astype(jnp.bfloat16), peak + jnp.log(totals))

    def attend_sequence(inputs):
        query_seq, key_seq, value_seq = inputs
        query_blocks = query_seq.reshape(block_count, block, local_heads, head_width)
        mixed, log_totals = lax.map(
            lambda item: attend_block(item[0], key_seq, value_seq, item[1]), (query_blocks, starts)
        )
        return (mixed.reshape(length, local_heads, head_width), log_totals)

    mixed_heads, log_totals = lax.map(attend_sequence, (heads_query, heads_key, heads_value))
    attention_result = lax.all_to_all(
        mixed_heads.reshape(seq_count, length, 1, group_width),
        "seq",
        split_axis=1,
        concat_axis=2,
        tiled=True,
    )
    attention_result = attention_result.reshape(rows, width)
    second_branch = residual_stream + jnp.dot(
        attention_result, full_output, preferred_element_type=jnp.float32
    )
    normed_two, factor_two = normalize(second_branch, ffn_gain)
    second_layer_norm = normed_two.astype(jnp.bfloat16)
    router_logits = jnp.dot(second_layer_norm, router, preferred_element_type=jnp.float32)
    probs = jax.nn.softmax(router_logits, axis=-1)
    token_ids = expert_ids.reshape(rows)
    onehot_int = (token_ids[:, None] == jnp.arange(experts)[None, :]).astype(jnp.int32)
    onehot_float = onehot_int.astype(jnp.float32)
    gate = jnp.sum(probs * onehot_float, axis=-1)
    slots = jnp.sum((jnp.cumsum(onehot_int, axis=0) - 1) * onehot_int, axis=-1)
    keep = (slots < capacity).astype(jnp.float32)
    slot_safe = jnp.minimum(slots, capacity - 1)
    send_rows = jnp.zeros((experts, capacity, width), jnp.bfloat16)
    send_rows = send_rows.at[token_ids, slot_safe].add(
        second_layer_norm * keep[:, None].astype(jnp.bfloat16)
    )
    received = lax.all_to_all(send_rows, "expert", split_axis=0, concat_axis=0, tiled=True)
    hidden = jnp.einsum("scd,df->scf", received, first_weight, preferred_element_type=jnp.float32)
    active = activation(hidden).astype(jnp.bfloat16)
    result = jnp.einsum(
        "scf,fd->scd", active, second_weight, preferred_element_type=jnp.float32
    ).astype(jnp.bfloat16)
    returned = lax.all_to_all(result, "expert", split_axis=0, concat_axis=0, tiled=True)
    returned, hidden_kept, received_kept = (returned, hidden, received)
    token_result = returned[token_ids, slot_safe].astype(jnp.float32) * keep[:, None]
    layer_out = (second_branch + gate[:, None] * token_result).astype(jnp.bfloat16)
    out_grad = cotangent.reshape(rows, width).astype(jnp.float32)
    gate_grad = jnp.sum(out_grad * token_result, axis=-1)
    logit_grad = probs * (onehot_float * gate_grad[:, None] - (gate * gate_grad)[:, None])
    router_grad = jnp.dot(
        second_layer_norm.astype(jnp.float32).T, logit_grad, precision=highest_precision
    )
    norm_two_grad = jnp.dot(logit_grad, router.astype(jnp.float32).T, precision=highest_precision)
    result_grad = (gate[:, None] * out_grad * keep[:, None]).astype(jnp.bfloat16)
    send_grads = (
        jnp.zeros((experts, capacity, width), jnp.bfloat16)
        .at[token_ids, slot_safe]
        .add(result_grad)
    )
    expert_side = lax.all_to_all(send_grads, "expert", split_axis=0, concat_axis=0, tiled=True)
    active_again = activation(hidden_kept).astype(jnp.bfloat16)
    second_grad = jnp.einsum(
        "scf,scd->fd", active_again, expert_side, preferred_element_type=jnp.float32
    )
    active_grad = jnp.einsum(
        "scd,fd->scf", expert_side, second_weight, preferred_element_type=jnp.float32
    )
    unused, gelu_pull = jax.vjp(activation, hidden_kept)
    hidden_grad = gelu_pull(active_grad)[0].astype(jnp.bfloat16)
    first_grad = jnp.einsum(
        "scd,scf->df", received_kept, hidden_grad, preferred_element_type=jnp.float32
    )
    rows_grad = jnp.einsum(
        "scf,df->scd", hidden_grad, first_weight, preferred_element_type=jnp.float32
    ).astype(jnp.bfloat16)
    back_grads = lax.all_to_all(rows_grad, "expert", split_axis=0, concat_axis=0, tiled=True)
    norm_two_grad = (
        norm_two_grad + back_grads[token_ids, slot_safe].astype(jnp.float32) * keep[:, None]
    )
    second_back, ffn_gain_grad = norm_back(norm_two_grad, second_branch, factor_two, ffn_gain)
    second_grad_total = out_grad + second_back
    grad_high = second_grad_total.astype(jnp.bfloat16)
    grad_rest = (second_grad_total - grad_high.astype(jnp.float32)).astype(jnp.bfloat16)
    output_weight_grad = jnp.dot(
        attention_result.T, grad_high, preferred_element_type=jnp.float32
    ) + jnp.dot(attention_result.T, grad_rest, preferred_element_type=jnp.float32)
    attended_grad = (
        jnp.dot(grad_high, full_output.T, preferred_element_type=jnp.float32)
        + jnp.dot(grad_rest, full_output.T, preferred_element_type=jnp.float32)
    ).astype(jnp.bfloat16)
    heads_grad = lax.all_to_all(
        to_groups(attended_grad), "seq", split_axis=2, concat_axis=1, tiled=True
    )
    heads_grad = heads_grad.reshape(seq_count, length, local_heads, head_width)
    span = length + block - 1

    def backward_sequence(inputs):
        query_seq, key_seq, value_seq, grad_seq, log_seq = inputs
        query_blocks = query_seq.reshape(block_count, block, local_heads, head_width)
        grad_blocks = grad_seq.reshape(block_count, block, local_heads, head_width)

        def step_block(carry, item):
            key_total, value_total, rel_total = carry
            query_block, grad_block, log_block, start = item
            bias = skew_bias(rel_heads, start, block, length)
            scores = (
                jnp.einsum("qhd,khd->hqk", query_block, key_seq, preferred_element_type=jnp.float32)
                * factor_scale
                + bias
            )
            weights = jnp.exp(scores - log_block)
            rounded = weights.astype(jnp.bfloat16)
            value_total = value_total + jnp.einsum(
                "hqk,qhd->khd", rounded, grad_block, preferred_element_type=jnp.float32
            )
            weight_grad = jnp.einsum(
                "qhd,khd->hqk", grad_block, value_seq, preferred_element_type=jnp.float32
            )
            inner = jnp.sum(weights * weight_grad, axis=-1, keepdims=True)
            score_grad = (weights * (weight_grad - inner)).astype(jnp.bfloat16)
            query_part = (
                jnp.einsum("hqk,khd->qhd", score_grad, key_seq, preferred_element_type=jnp.float32)
                * factor_scale
            ).astype(jnp.bfloat16)
            key_total = (
                key_total
                + jnp.einsum(
                    "hqk,qhd->khd", score_grad, query_block, preferred_element_type=jnp.float32
                )
                * factor_scale
            )
            sums = diagonal_sums(score_grad.astype(jnp.float32), block, length)
            offset = length - block - start
            current = lax.dynamic_slice_in_dim(rel_total, offset, span, 1)
            rel_total = lax.dynamic_update_slice_in_dim(rel_total, current + sums, offset, 1)
            return ((key_total, value_total, rel_total), query_part)

        start_carry = (
            jnp.zeros((length, local_heads, head_width), jnp.float32),
            jnp.zeros((length, local_heads, head_width), jnp.float32),
            jnp.zeros((local_heads, 2 * length - 1), jnp.float32),
        )
        totals, query_parts = lax.scan(
            step_block, start_carry, (query_blocks, grad_blocks, log_seq, starts)
        )
        return (
            query_parts.reshape(length, local_heads, head_width),
            totals[0].astype(jnp.bfloat16),
            totals[1].astype(jnp.bfloat16),
            totals[2],
        )

    query_back, key_back, value_back, rel_back = lax.map(
        backward_sequence, (heads_query, heads_key, heads_value, heads_grad, log_totals)
    )
    table_local = jnp.dot(bucket_onehot.T, jnp.sum(rel_back, axis=0).T, precision=highest_precision)
    table_grad = lax.dynamic_update_slice_in_dim(
        jnp.zeros((bucket_count, heads_all), jnp.float32), table_local, head_start, 1
    )
    query_tok, key_tok, value_tok = (
        lax.all_to_all(
            query_back.reshape(seq_count, length, 1, group_width),
            "seq",
            split_axis=1,
            concat_axis=2,
            tiled=True,
        ),
        lax.all_to_all(
            key_back.reshape(seq_count, length, 1, group_width),
            "seq",
            split_axis=1,
            concat_axis=2,
            tiled=True,
        ),
        lax.all_to_all(
            value_back.reshape(seq_count, length, 1, group_width),
            "seq",
            split_axis=1,
            concat_axis=2,
            tiled=True,
        ),
    )
    query_tok = query_tok.reshape(rows, width)
    key_tok = key_tok.reshape(rows, width)
    value_tok = value_tok.reshape(rows, width)
    query_weight_grad = jnp.dot(first_layer_norm.T, query_tok, preferred_element_type=jnp.float32)
    key_weight_grad = jnp.dot(first_layer_norm.T, key_tok, preferred_element_type=jnp.float32)
    value_weight_grad = jnp.dot(first_layer_norm.T, value_tok, preferred_element_type=jnp.float32)
    norm_one_grad = jnp.dot(query_tok, full_query.T, preferred_element_type=jnp.float32)
    norm_one_grad = norm_one_grad + jnp.dot(key_tok, full_key.T, preferred_element_type=jnp.float32)
    norm_one_grad = norm_one_grad + jnp.dot(
        value_tok, full_value.T, preferred_element_type=jnp.float32
    )
    first_back, attn_gain_grad = norm_back(norm_one_grad, residual_stream, factor_one, attn_gain)
    input_grad = second_grad_total + first_back
    dense_query, dense_key, dense_value, dense_output = (
        lax.psum_scatter(query_weight_grad, ("dp", "expert"), scatter_dimension=0, tiled=True),
        lax.psum_scatter(key_weight_grad, ("dp", "expert"), scatter_dimension=0, tiled=True),
        lax.psum_scatter(value_weight_grad, ("dp", "expert"), scatter_dimension=0, tiled=True),
        lax.psum_scatter(output_weight_grad, ("dp", "expert"), scatter_dimension=0, tiled=True),
    )
    summed = across_replicas(
        first_grad[None], second_grad[None], dense_query, dense_key, dense_value, dense_output
    )
    first_share, second_share = expert_shards(summed[0], summed[1])
    attn_gain_total, ffn_gain_total, router_total, table_total = lax.psum(
        (attn_gain_grad, ffn_gain_grad, router_grad, table_grad), ("dp", "expert", "seq")
    )
    return (
        layer_out.reshape(seq_count, piece, width),
        input_grad.reshape(seq_count, piece, width),
        attn_gain_total,
        summed[2],
        summed[3],
        summed[4],
        summed[5],
        table_total,
        ffn_gain_total,
        router_total,
        first_share,
        second_share,
    )


def solution(mesh):
    placed = (
        P(("dp", "expert"), "seq", None),
        P(),
        P(("dp", "expert"), None),
        P(("dp", "expert"), None),
        P(("dp", "expert"), None),
        P(("dp", "expert"), None),
        P(),
        P(),
        P(),
        P(),
        P("expert", "dp", None),
        P("expert", "dp", None),
        P(("dp", "expert"), "seq"),
        P(("dp", "expert"), "seq", None),
    )
    return jax.shard_map(
        local,
        mesh=mesh,
        in_specs=placed,
        out_specs=(
            P(("dp", "expert"), "seq", None),
            P(("dp", "expert"), "seq", None),
            P(),
            P(("dp", "expert"), None),
            P(("dp", "expert"), None),
            P(("dp", "expert"), None),
            P(("dp", "expert"), None),
            P(),
            P(),
            P(),
            P("expert", "dp", None),
            P("expert", "dp", None),
        ),
        check_vma=False,
    )
```

profile of v0, /device:TPU:0, one launch (start us, length us, event | category | flops | bytes accessed | tf_op | source)
XLA Modules:
  0.0 2276.3 jit_solution(12815551081731040078)
XLA Ops:
  14.5 22.2 all-gather.11.cloned.1.call-done
  44.7 18.0 all-gather.9.cloned.1.call-done
  70.7 18.0 all-gather.7.cloned.1.call-done
  102.7 14.5 all-to-all-done
  120.3 479.0 %while.96 = (s32[]{:T(128)}, bf16[2,1024,3,64]{1,3,2,0:T(8,128)(2,1)}, f32[2,2,3,512,1]{3,2,1,4,0:T(4,128)}, bf16[2,1024,3,64]{1,3,2,0:T(8,128)(2,1)}, bf16[2,10...) while((s32[]{:T(128)}, ...), condition=%wide.region_6.7_spmd.clone, body=%wide.region_1.6_spmd.clone.sunk | while | flops 415332864 | bytes 149336672 | solution.py:164
  137.9 226.0 %while.99 = (s32[]{:T(128)}, bf16[2,512,3,64]{1,3,2,0:T(8,128)(2,1)}, f32[2,3,512,1]{2,1,3,0:T(4,128)S(1)}, bf16[2,512,3,64]{1,3,2,0:T(8,128)(2,1)}, bf16[1024,3...) while((s32[]{:T(128)}, ...), condition=%wide.region_5.5_spmd, body=%wide.region_2.4_spmd.sunk | while | flops 415332864 | bytes 142815504 | solution.py:159
  145.3 15.2 reshape.460
  160.6 14.5 reshape.461
  195.1 48.5 %rev.26 = f32[3,512,1024]{2,1,0:T(8,128)} reverse(f32[3,512,1024]{2,1,0:T(8,128)} %slice.46), dimensions={1} | reverse | bytes 12582912 | tf_op jit(solution)/shard_map/while/body/eval_jaxpr/while/body/eval_jaxpr/jit(_flip)/rev | solution.py:37
  259.0 15.2 reshape.460
  274.2 13.2 reshape.461
  307.4 48.5 %rev.26 = f32[3,512,1024]{2,1,0:T(8,128)} reverse(f32[3,512,1024]{2,1,0:T(8,128)} %slice.46), dimensions={1} | reverse | bytes 12582912 | tf_op jit(solution)/shard_map/while/body/eval_jaxpr/while/body/eval_jaxpr/jit(_flip)/rev | solution.py:37
  371.4 224.6 %while.99 = (s32[]{:T(128)}, bf16[2,512,3,64]{1,3,2,0:T(8,128)(2,1)}, f32[2,3,512,1]{2,1,3,0:T(4,128)S(1)}, bf16[2,512,3,64]{1,3,2,0:T(8,128)(2,1)}, bf16[1024,3...) while((s32[]{:T(128)}, ...), condition=%wide.region_5.5_spmd, body=%wide.region_2.4_spmd.sunk | while | flops 415332864 | bytes 142815504 | solution.py:159
  378.9 15.2 reshape.460
  394.0 13.2 reshape.461
  427.2 48.5 %rev.26 = f32[3,512,1024]{2,1,0:T(8,128)} reverse(f32[3,512,1024]{2,1,0:T(8,128)} %slice.46), dimensions={1} | reverse | bytes 12582912 | tf_op jit(solution)/shard_map/while/body/eval_jaxpr/while/body/eval_jaxpr/jit(_flip)/rev | solution.py:37
  491.1 15.2 reshape.460
  506.3 13.2 reshape.461
  539.5 48.5 %rev.26 = f32[3,512,1024]{2,1,0:T(8,128)} reverse(f32[3,512,1024]{2,1,0:T(8,128)} %slice.46), dimensions={1} | reverse | bytes 12582912 | tf_op jit(solution)/shard_map/while/body/eval_jaxpr/while/body/eval_jaxpr/jit(_flip)/rev | solution.py:37
  607.9 23.6 %all-to-all-done.3 = bf16[2,1024,1,192]{3,0,2,1:T(2,128)(2,1)S(1)} async-done(((bf16[2,1024,1,192]{3,0,2,1:T(2,128)(2,1)}), bf16[2,1024,1,192]{3,0,2,1:T(2,128)(2,1)S(1)}, u32[]{:S(2)}, u32[]{:S(2)}) %all-to-all-start.3) | async-done | bytes 786464 | tf_op jit(solution)/shard_map/all_to_all | solution.py:165
  640.8 75.6 %scatter_fusion = bf16[2,320,768]{2,1,0:T(8,128)(2,1)} fusion(bf16[2,320,768]{2,1,0:T(8,128)(2,1)} %broadcast.344.clone, s32[512]{0:T(512)S(1)} %bitcast.368, bf16[512,768]{1,0:T(8,128)(2,1)} %get-tuple-element.896), kind=kCustom, calls=%fused_computation.2 | custom fusion | flops 393216 | bytes 2363392 | tf_op jit(solution)/shard_map/scatter-add | solution.py:188
  722.8 75.5 %scatter_fusion.1 = bf16[2,320,768]{2,1,0:T(8,128)(2,1)} fusion(bf16[2,320,768]{2,1,0:T(8,128)(2,1)} %broadcast.344.clone.1, s32[512]{0:T(512)S(1)} %bitcast.369, bf16[512,768]{1,0:T(8,128)(2,1)S(1)} %fusion.60), kind=kCustom, calls=%fused_computation.3 | custom fusion | flops 393216 | bytes 2363392 | tf_op jit(solution)/shard_map/scatter-add | solution.py:212
  813.7 18.9 multiply_convert_fusion.1
  843.9 10.7 add_convert_fusion
  903.8 16.3 all-to-all-done.8
  925.2 940.9 %while.98 = (s32[]{:T(128)}, bf16[2,1024,3,64]{1,3,2,0:T(8,128)(2,1)}, bf16[2,1024,3,64]{1,3,2,0:T(8,128)(2,1)}, bf16[2,1024,3,64]{1,3,2,0:T(8,128)(2,1)}, f32[2...) while((s32[]{:T(128)}, ...), condition=%wide.region_23.24_spmd.clone, body=%wide.region_18.23_spmd.clone.sunk | while | flops 1024717824 | bytes 309597024 | solution.py:307
  954.9 441.6 %while.100 = (s32[]{:T(128)}, f32[1024,3,64]{0,2,1:T(8,128)}, f32[1024,3,64]{0,2,1:T(8,128)}, f32[3,2047]{1,0:T(4,128)}, bf16[2,512,3,64]{1,3,2,0:T(8,128)(2,1)}...) while((s32[]{:T(128)}, f32[1024,3,64]{0,2,1:T(8,128)}, ...), condition=%wide.region_22.22_spmd.clone, body=%wide.region_19.21_spmd.clone.sunk | while | flops 1024324608 | bytes 298275392 | solution.py:297
  966.4 15.2 reshape.456
  981.6 13.2 reshape.457
  1014.7 48.6 %rev.24 = f32[3,512,1024]{2,1,0:T(8,128)} reverse(f32[3,512,1024]{2,1,0:T(8,128)} %slice.44), dimensions={1} | reverse | bytes 12582912 | tf_op jit(solution)/shard_map/while/body/eval_jaxpr/while/body/eval_jaxpr/jit(_flip)/rev | solution.py:37
  1079.3 31.8 %rev.25 = f32[3,512,1024]{2,1,0:T(8,128)} reverse(bf16[3,512,1024]{2,1,0:T(8,128)(2,1)S(1)} %multiply_convert_fusion.5), dimensions={1} | reverse | bytes 9437184 | tf_op jit(solution)/shard_map/while/body/eval_jaxpr/while/body/eval_jaxpr/jit(_flip)/rev | solution.py:43
  1115.1 19.9 copy.167
  1140.8 13.2 reshape.458
  1154.0 15.7 reshape.459
  1186.6 15.2 reshape.456
  1201.8 13.2 reshape.457
  1235.0 48.6 %rev.24 = f32[3,512,1024]{2,1,0:T(8,128)} reverse(f32[3,512,1024]{2,1,0:T(8,128)} %slice.44), dimensions={1} | reverse | bytes 12582912 | tf_op jit(solution)/shard_map/while/body/eval_jaxpr/while/body/eval_jaxpr/jit(_flip)/rev | solution.py:37
  1300.7 31.8 %rev.25 = f32[3,512,1024]{2,1,0:T(8,128)} reverse(bf16[3,512,1024]{2,1,0:T(8,128)(2,1)S(1)} %multiply_convert_fusion.5), dimensions={1} | reverse | bytes 9437184 | tf_op jit(solution)/shard_map/while/body/eval_jaxpr/while/body/eval_jaxpr/jit(_flip)/rev | solution.py:43
  1336.5 19.9 copy.167
  1362.2 13.2 reshape.458
  1375.4 15.7 reshape.459
  1410.1 441.6 %while.100 = (s32[]{:T(128)}, f32[1024,3,64]{0,2,1:T(8,128)}, f32[1024,3,64]{0,2,1:T(8,128)}, f32[3,2047]{1,0:T(4,128)}, bf16[2,512,3,64]{1,3,2,0:T(8,128)(2,1)}...) while((s32[]{:T(128)}, f32[1024,3,64]{0,2,1:T(8,128)}, ...), condition=%wide.region_22.22_spmd.clone, body=%wide.region_19.21_spmd.clone.sunk | while | flops 1024324608 | bytes 298275392 | solution.py:297
  1421.6 15.2 reshape.456
  1436.8 13.2 reshape.457
  1469.9 48.6 %rev.24 = f32[3,512,1024]{2,1,0:T(8,128)} reverse(f32[3,512,1024]{2,1,0:T(8,128)} %slice.44), dimensions={1} | reverse | bytes 12582912 | tf_op jit(solution)/shard_map/while/body/eval_jaxpr/while/body/eval_jaxpr/jit(_flip)/rev | solution.py:37
  1534.5 31.8 %rev.25 = f32[3,512,1024]{2,1,0:T(8,128)} reverse(bf16[3,512,1024]{2,1,0:T(8,128)(2,1)S(1)} %multiply_convert_fusion.5), dimensions={1} | reverse | bytes 9437184 | tf_op jit(solution)/shard_map/while/body/eval_jaxpr/while/body/eval_jaxpr/jit(_flip)/rev | solution.py:43
  1570.3 19.9 copy.167
  1596.0 13.2 reshape.458
  1609.2 15.7 reshape.459
  1641.8 15.2 reshape.456
  1657.0 13.2 reshape.457
  1690.2 48.6 %rev.24 = f32[3,512,1024]{2,1,0:T(8,128)} reverse(f32[3,512,1024]{2,1,0:T(8,128)} %slice.44), dimensions={1} | reverse | bytes 12582912 | tf_op jit(solution)/shard_map/while/body/eval_jaxpr/while/body/eval_jaxpr/jit(_flip)/rev | solution.py:37
  1755.9 31.8 %rev.25 = f32[3,512,1024]{2,1,0:T(8,128)} reverse(bf16[3,512,1024]{2,1,0:T(8,128)(2,1)S(1)} %multiply_convert_fusion.5), dimensions={1} | reverse | bytes 9437184 | tf_op jit(solution)/shard_map/while/body/eval_jaxpr/while/body/eval_jaxpr/jit(_flip)/rev | solution.py:43
  1791.7 19.9 copy.167
  1817.4 13.2 reshape.458
  1830.6 15.7 reshape.459
  1874.7 23.7 %all-to-all-done.11 = bf16[2,1024,1,192]{3,0,2,1:T(2,128)(2,1)S(1)} async-done(((bf16[2,1024,1,192]{3,0,2,1:T(2,128)(2,1)}), bf16[2,1024,1,192]{3,0,2,1:T(2,128)(2,1)S(1)}, u32[]{:S(2)}, u32[]{:S(2)}) %all-to-all-start.11) | async-done | bytes 786464 | tf_op jit(solution)/shard_map/all_to_all | solution.py:329
  1906.1 28.4 %all_to_all.140 = bf16[2,1024,1,192]{3,0,2,1:T(2,128)(2,1)} all-to-all(bf16[2,1024,1,192]{3,0,2,1:T(2,128)(2,1)S(1)} %copy.120), channel_id=1, replica_groups=mesh['dp'=4,'expert'=2,'seq'=4] {'seq'}, dimensions={1} | all-to-all | bytes 1572864 | tf_op jit(solution)/shard_map/all_to_all | solution.py:322
  1943.3 27.9 %all_to_all.141 = bf16[2,1024,1,192]{3,0,2,1:T(2,128)(2,1)} all-to-all(bf16[2,1024,1,192]{3,0,2,1:T(2,128)(2,1)S(1)} %copy.118), channel_id=1, replica_groups=mesh['dp'=4,'expert'=2,'seq'=4] {'seq'}, dimensions={1} | all-to-all | bytes 1572864 | tf_op jit(solution)/shard_map/all_to_all | solution.py:315
  2001.3 35.3 %reduce-scatter.7.cloned.1.call-done = f32[96,768]{1,0:T(8,128)} async-done(((f32[768,768]{1,0:T(8,128)}), f32[96,768]{1,0:T(8,128)}) %reduce-scatter.7.cloned.1.call-update) | async-done | bytes 294928 | tf_op jit(solution)/shard_map/reduce_scatter | solution.py:351
  2038.3 48.8 %reduce-scatter.17.cloned.1.call-done = bf16[1,768,768]{2,1,0:T(8,128)(2,1)} async-done(((bf16[1,3072,768]{2,1,0:T(8,128)(2,1)}), bf16[1,768,768]{2,1,0:T(8,128)(2,1)}) %reduce-scatter.17.cloned.1.call-update) | async-done | bytes 1179664 | tf_op jit(solution)/shard_map/reduce_scatter | solution.py:54
  2087.1 50.5 %reduce-scatter.15.cloned.1.call-done = bf16[1,192,3072]{2,1,0:T(8,128)(2,1)} async-done(((bf16[1,768,3072]{2,1,0:T(8,128)(2,1)}), bf16[1,192,3072]{2,1,0:T(8,128)(2,1)}) %reduce-scatter.15.cloned.1.call-update) | async-done | bytes 1179664 | tf_op jit(solution)/shard_map/reduce_scatter | solution.py:51
  2147.0 43.4 %all-reduce.3 = (f32[768]{0:T(1024)}, f32[32,12]{0,1:T(8,128)}, f32[768]{0:T(1024)}, f32[768,2]{0,1:T(2,128)}) all-reduce(f32[768]{0:T(1024)S(1)} %get-tuple-element.806, f32[32,12]{0,1:T(8,128)S(1)} %dynamic_update_slice.68, f32[768]{0:T(1024)S(1)} %copy-done.54, ...), channel_id=1, replica_groups=mesh['dp'=4,'expert'=2,'seq'=4] {'dp','expert','seq'}, use_global_device_ids=true, to_apply=%region_26.27 | all-reduce | flops 3456 | bytes 27648 | tf_op jit(solution)/shard_map/psum | solution.py:360
  2193.4 65.0 %all-reduce.7.cloned.1.call-done = (bf16[96,768]{1,0:T(8,128)(2,1)}, bf16[96,768]{1,0:T(8,128)(2,1)}, bf16[96,768]{1,0:T(8,128)(2,1)}, bf16[96,768]{1,0:T(8,128)...) async-done(((bf16[96,768]{1,0:T(8,128)(2,1)}, bf16[96,768]{1,0:T(8,128)(2,1)}, bf16[96,768]{1,0:T(8,128)(2,1)}, bf16[96,768]{1,0:T(8,128)(2,1)}, ...) | async-done | bytes 2949136 | tf_op jit(solution)/shard_map/psum | solution.py:64
  (582 shorter events, 651.0 us)
Async XLA Ops:
  7.2 90.7 %copy-start = (f32[32,12]{0,1:T(8,128)S(1)}, f32[32,12]{0,1:T(8,128)}, u32[]{:S(2)}) copy-start(f32[32,12]{0,1:T(8,128)} %param.28) | copy-start | bytes 4612
  7.2 29.5 %all-gather.11.cloned.1.call-start = ((), (), s32[]{:S(2)}) async-start(), calls=%async_computation.20 | async-start | bytes 1327104 | tf_op jit(solution)/shard_map/all_gather | solution.py:103
  7.9 54.7 %all-gather.9.cloned.1.call-start = ((), (), s32[]{:S(2)}) async-start(), calls=%async_computation.19 | async-start | bytes 1327104 | tf_op jit(solution)/shard_map/all_gather | solution.py:102
  8.7 80.0 %all-gather.7.cloned.1.call-start = ((), (), s32[]{:S(2)}) async-start(), calls=%async_computation.18 | async-start | bytes 1327104 | tf_op jit(solution)/shard_map/all_gather | solution.py:101
  9.4 626.7 %all-gather.13.cloned.1.call-start = ((), (), s32[]{:S(2)}) async-start(), calls=%async_computation.21 | async-start | bytes 1327104 | tf_op jit(solution)/shard_map/all_gather | solution.py:104
  10.0 792.8 %all-gather.15.cloned.1.call-start = ((), (), s32[]{:S(2)}) async-start(), calls=%async_computation.22 | async-start | bytes 5898240 | tf_op jit(solution)/shard_map/all_gather | solution.py:107
  40.1 26.0 %all-to-all-start.2 = ((bf16[2,256,4,192]{1,0,3,2:T(2,128)(2,1)}), bf16[2,256,4,192]{1,0,3,2:T(2,128)(2,1)S(1)}, u32[]{:S(2)}, u32[]{:S(2)}) async-start(bf16[2,256,4,192]{1,0,3,2:T(2,128)(2,1)} %reshape.382), calls=%async_computation.2 | async-start | bytes 1572864 | tf_op jit(solution)/shard_map/all_to_all | solution.py:131
  66.1 26.0 %all-to-all-start.1 = ((bf16[2,256,4,192]{1,0,3,2:T(2,128)(2,1)}), bf16[2,256,4,192]{1,0,3,2:T(2,128)(2,1)S(1)}, u32[]{:S(2)}, u32[]{:S(2)}) async-start(bf16[2,256,4,192]{1,0,3,2:T(2,128)(2,1)} %reshape.380), calls=%async_computation.1 | async-start | bytes 1572864 | tf_op jit(solution)/shard_map/all_to_all | solution.py:130
  70.7 26.6 %copy-start.52 = (s32[2,256]{1,0:T(2,128)S(1)}, s32[2,256]{1,0:T(2,128)}, u32[]{:S(2)}) copy-start(s32[2,256]{1,0:T(2,128)} %param.34) | copy-start | bytes 6148
  70.7 27.2 %copy-start.58 = (s32[2047]{0:T(1024)S(1)}, s32[2047]{0:T(1024)}, u32[]{:S(2)}) copy-start(s32[2047]{0:T(1024)} %param.29) | copy-start | bytes 24568
  92.1 25.1 %all-to-all-start = ((bf16[2,256,4,192]{1,0,3,2:T(2,128)(2,1)}), bf16[2,256,4,192]{1,0,3,2:T(2,128)(2,1)S(1)}, u32[]{:S(2)}, u32[]{:S(2)}) async-start(bf16[2,256,4,192]{1,0,3,2:T(2,128)(2,1)} %reshape.378), calls=%async_computation | async-start | bytes 1572864 | tf_op jit(solution)/shard_map/all_to_all | solution.py:129
  96.7 735.9 %all-gather.17.cloned.1.call-start = ((), (), s32[]{:S(2)}) async-start(), calls=%async_computation.23 | async-start | bytes 5898240 | tf_op jit(solution)/shard_map/all_gather | solution.py:108
  120.3 486.4 %copy-start.57 = (s32[4,128]{1,0:T(4,128)S(1)}, s32[4,128]{1,0:T(4,128)}, u32[]{:S(2)}) copy-start(s32[4,128]{1,0:T(4,128)} %eq.45) | copy-start | bytes 6148
  120.3 486.4 %copy-start.53 = (s32[2,256]{1,0:T(2,128)S(1)}, s32[2,256]{1,0:T(2,128)}, u32[]{:S(2)}) copy-start(s32[2,256]{1,0:T(2,128)} %param.34) | copy-start | bytes 6148
  137.9 226.0 %copy-start.37 = (f32[2,2,3,512,1]{3,2,1,4,0:T(4,128)S(1)}, f32[2,2,3,512,1]{3,2,1,4,0:T(4,128)}, u32[]{:S(2)}) copy-start(f32[2,2,3,512,1]{3,2,1,4,0:T(4,128)} %get-tuple-element.1333) | copy-start | bytes 73732 | tf_op jit(solution)/shard_map/while
  195.1 48.5 %copy-start.10 = (bf16[2,512,3,64]{1,3,2,0:T(8,128)(2,1)S(1)}, bf16[2,512,3,64]{1,3,2,0:T(8,128)(2,1)}, u32[]{:S(2)}) copy-start(bf16[2,512,3,64]{1,3,2,0:T(8,128)(2,1)} %get-tuple-element.1307) | copy-start | bytes 1179652 | tf_op jit(solution)/shard_map/while/body/eval_jaxpr/while
  307.4 48.5 %copy-start.10 = (bf16[2,512,3,64]{1,3,2,0:T(8,128)(2,1)S(1)}, bf16[2,512,3,64]{1,3,2,0:T(8,128)(2,1)}, u32[]{:S(2)}) copy-start(bf16[2,512,3,64]{1,3,2,0:T(8,128)(2,1)} %get-tuple-element.1307) | copy-start | bytes 1179652 | tf_op jit(solution)/shard_map/while/body/eval_jaxpr/while
  371.4 224.6 %copy-start.37 = (f32[2,2,3,512,1]{3,2,1,4,0:T(4,128)S(1)}, f32[2,2,3,512,1]{3,2,1,4,0:T(4,128)}, u32[]{:S(2)}) copy-start(f32[2,2,3,512,1]{3,2,1,4,0:T(4,128)} %get-tuple-element.1333) | copy-start | bytes 73732 | tf_op jit(solution)/shard_map/while
  427.2 48.5 %copy-start.10 = (bf16[2,512,3,64]{1,3,2,0:T(8,128)(2,1)S(1)}, bf16[2,512,3,64]{1,3,2,0:T(8,128)(2,1)}, u32[]{:S(2)}) copy-start(bf16[2,512,3,64]{1,3,2,0:T(8,128)(2,1)} %get-tuple-element.1307) | copy-start | bytes 1179652 | tf_op jit(solution)/shard_map/while/body/eval_jaxpr/while
  539.5 48.5 %copy-start.10 = (bf16[2,512,3,64]{1,3,2,0:T(8,128)(2,1)S(1)}, bf16[2,512,3,64]{1,3,2,0:T(8,128)(2,1)}, u32[]{:S(2)}) copy-start(bf16[2,512,3,64]{1,3,2,0:T(8,128)(2,1)} %get-tuple-element.1307) | copy-start | bytes 1179652 | tf_op jit(solution)/shard_map/while/body/eval_jaxpr/while
  599.3 36.8 %copy-start.17 = (bf16[2,256,768]{2,1,0:T(8,128)(2,1)S(1)}, bf16[2,256,768]{2,1,0:T(8,128)(2,1)}, u32[]{:S(2)}) copy-start(bf16[2,256,768]{2,1,0:T(8,128)(2,1)} %param.22) | copy-start | bytes 2359300
  603.0 35.3 %copy-start.45 = (f32[768]{0:T(1024)S(1)}, f32[768]{0:T(1024)}, u32[]{:S(2)}) copy-start(f32[768]{0:T(1024)} %param.30) | copy-start | bytes 9220
  603.0 28.5 %all-to-all-start.3 = ((bf16[2,1024,1,192]{3,0,2,1:T(2,128)(2,1)}), bf16[2,1024,1,192]{3,0,2,1:T(2,128)(2,1)S(1)}, u32[]{:S(2)}, u32[]{:S(2)}) async-start(bf16[2,1024,1,192]{3,0,2,1:T(2,128)(2,1)} %copy.111), calls=%async_computation.3 | async-start | bytes 2097152 | tf_op jit(solution)/shard_map/all_to_all | solution.py:165
  606.7 278.0 %copy-start.41 = (s32[1,2,2,128]{3,1,2,0:T(2,128)}, s32[1,2,2,128]{3,1,2,0:T(2,128)S(1)}, u32[]{:S(2)}) copy-start(s32[1,2,2,128]{3,1,2,0:T(2,128)S(1)} %copy.137) | copy-start | bytes 6148
  638.3 78.1 %copy-start.19 = (f32[512,768]{1,0:T(8,128)}, f32[512,768]{1,0:T(8,128)S(1)}, u32[]{:S(2)}) copy-start(f32[512,768]{1,0:T(8,128)S(1)} %get-tuple-element.919) | copy-start | bytes 4718596
  639.7 80.3 %copy-start.26 = (bf16[512,768]{1,0:T(8,128)(2,1)}, bf16[512,768]{1,0:T(8,128)(2,1)S(1)}, u32[]{:S(2)}) copy-start(bf16[512,768]{1,0:T(8,128)(2,1)S(1)} %get-tuple-element.897) | copy-start | bytes 2359300
  640.8 79.2 %copy-start.55 = (bf16[768,2]{0,1:T(2,128)(2,1)S(1)}, bf16[768,2]{0,1:T(2,128)(2,1)}, u32[]{:S(2)}) copy-start(bf16[768,2]{0,1:T(2,128)(2,1)} %param.31) | copy-start | bytes 9220
  716.4 81.9 %all-to-all-start.4 = ((bf16[2,320,768]{2,1,0:T(8,128)(2,1)}), bf16[2,320,768]{2,1,0:T(8,128)(2,1)S(1)}, u32[]{:S(2)}, u32[]{:S(2)}) async-start(bf16[2,320,768]{2,1,0:T(8,128)(2,1)} %scatter_fusion), calls=%async_computation.4 | async-start | bytes 1966080 | tf_op jit(solution)/shard_map/all_to_all | solution.py:191
  720.4 164.3 %copy-start.46 = (f32[512,2]{0,1:T(2,128)}, f32[512,2]{0,1:T(2,128)S(1)}, u32[]{:S(2)}) copy-start(f32[512,2]{0,1:T(2,128)S(1)} %get-tuple-element.901) | copy-start | bytes 12292
  798.4 12.2 copy-start.35
  798.4 41.9 %all-to-all-start.6 = ((bf16[2,320,768]{2,1,0:T(8,128)(2,1)}), bf16[2,320,768]{2,1,0:T(8,128)(2,1)}, u32[]{:S(2)}, u32[]{:S(2)}) async-start(bf16[2,320,768]{2,1,0:T(8,128)(2,1)} %scatter_fusion.1), calls=%async_computation.6 | async-start | bytes 1966080 | tf_op jit(solution)/shard_map/all_to_all | solution.py:214
  840.3 22.8 %all-to-all-start.5 = ((bf16[2,320,768]{2,1,0:T(8,128)(2,1)}), bf16[2,320,768]{2,1,0:T(8,128)(2,1)S(1)}, u32[]{:S(2)}, u32[]{:S(2)}) async-start(bf16[2,320,768]{2,1,0:T(8,128)(2,1)} %fusion.75), calls=%async_computation.5 | async-start | bytes 1966080 | tf_op jit(solution)/shard_map/all_to_all | solution.py:197
  863.1 17.0 all-to-all-start.7
  875.7 12.7 copy-start.48
  875.7 12.6 copy-start.50
  896.8 23.3 %all-to-all-start.8 = ((bf16[2,256,4,192]{1,0,3,2:T(2,128)(2,1)}), bf16[2,256,4,192]{1,0,3,2:T(2,128)(2,1)S(1)}, u32[]{:S(2)}, u32[]{:S(2)}) async-start(bf16[2,256,4,192]{1,0,3,2:T(2,128)(2,1)} %reshape.389), calls=%async_computation.8 | async-start | bytes 1572864 | tf_op jit(solution)/shard_map/all_to_all | solution.py:245
  900.3 1095.9 %reduce-scatter.13.cloned.1.call-start = ((), (), s32[]{:S(2)}) async-start(), calls=%async_computation.27 | async-start | bytes 2654208 | tf_op jit(solution)/shard_map/reduce_scatter | solution.py:354
  925.2 948.1 %copy-start.39 = (f32[768]{0:T(1024)S(1)}, f32[768]{0:T(1024)}, u32[]{:S(2)}) copy-start(f32[768]{0:T(1024)} %param.23) | copy-start | bytes 9220
  925.2 948.1 %copy-start.56 = (f32[2,256]{1,0:T(2,128)S(1)}, f32[2,256]{1,0:T(2,128)}, u32[]{:S(2)}) copy-start(f32[2,256]{1,0:T(2,128)} %get-tuple-element.912) | copy-start | bytes 6148
  1014.7 48.6 %copy-start.4 = (bf16[2,512,3,64]{1,3,2,0:T(8,128)(2,1)S(1)}, bf16[2,512,3,64]{1,3,2,0:T(8,128)(2,1)}, u32[]{:S(2)}) copy-start(bf16[2,512,3,64]{1,3,2,0:T(8,128)(2,1)} %get-tuple-element.1266) | copy-start | bytes 1179652 | tf_op jit(solution)/shard_map/while/body/eval_jaxpr/while
  1175.1 11.5 copy-start.6
  1175.1 11.5 copy-start.8
  1235.0 48.6 %copy-start.4 = (bf16[2,512,3,64]{1,3,2,0:T(8,128)(2,1)S(1)}, bf16[2,512,3,64]{1,3,2,0:T(8,128)(2,1)}, u32[]{:S(2)}) copy-start(bf16[2,512,3,64]{1,3,2,0:T(8,128)(2,1)} %get-tuple-element.1266) | copy-start | bytes 1179652 | tf_op jit(solution)/shard_map/while/body/eval_jaxpr/while
  1469.9 48.6 %copy-start.4 = (bf16[2,512,3,64]{1,3,2,0:T(8,128)(2,1)S(1)}, bf16[2,512,3,64]{1,3,2,0:T(8,128)(2,1)}, u32[]{:S(2)}) copy-start(bf16[2,512,3,64]{1,3,2,0:T(8,128)(2,1)} %get-tuple-element.1266) | copy-start | bytes 1179652 | tf_op jit(solution)/shard_map/while/body/eval_jaxpr/while
  1630.3 11.5 copy-start.6
  1690.2 48.6 %copy-start.4 = (bf16[2,512,3,64]{1,3,2,0:T(8,128)(2,1)S(1)}, bf16[2,512,3,64]{1,3,2,0:T(8,128)(2,1)}, u32[]{:S(2)}) copy-start(bf16[2,512,3,64]{1,3,2,0:T(8,128)(2,1)} %get-tuple-element.1266) | copy-start | bytes 1179652 | tf_op jit(solution)/shard_map/while/body/eval_jaxpr/while
  1869.7 28.7 %all-to-all-start.11 = ((bf16[2,1024,1,192]{3,0,2,1:T(2,128)(2,1)}), bf16[2,1024,1,192]{3,0,2,1:T(2,128)(2,1)S(1)}, u32[]{:S(2)}, u32[]{:S(2)}) async-start(bf16[2,1024,1,192]{3,0,2,1:T(2,128)(2,1)} %copy.123), calls=%async_computation.11 | async-start | bytes 2097152 | tf_op jit(solution)/shard_map/all_to_all | solution.py:329
  1873.2 124.8 %reduce-scatter.11.cloned.1.call-start = ((), (), s32[]{:S(2)}) async-start(), calls=%async_computation.26 | async-start | bytes 2654208 | tf_op jit(solution)/shard_map/reduce_scatter | solution.py:353
  1903.6 96.0 %reduce-scatter.9.cloned.1.call-start = ((), (), s32[]{:S(2)}) async-start(), calls=%async_computation.25 | async-start | bytes 2654208 | tf_op jit(solution)/shard_map/reduce_scatter | solution.py:352
  1940.8 95.9 %reduce-scatter.7.cloned.1.call-start = ((), (), s32[]{:S(2)}) async-start(), calls=%async_computation.24 | async-start | bytes 2654208 | tf_op jit(solution)/shard_map/reduce_scatter | solution.py:351
  1978.4 108.6 %reduce-scatter.17.cloned.1.call-start = ((), (), s32[]{:S(2)}) async-start(), calls=%async_computation.29 | async-start | bytes 5898240 | tf_op jit(solution)/shard_map/reduce_scatter | solution.py:54
  1986.9 150.6 %reduce-scatter.15.cloned.1.call-start = ((), (), s32[]{:S(2)}) async-start(), calls=%async_computation.28 | async-start | bytes 5898240 | tf_op jit(solution)/shard_map/reduce_scatter | solution.py:51
  1996.1 141.5 %copy-start.44 = (f32[1,2,2,128]{3,1,2,0:T(2,128)S(1)}, f32[1,2,2,128]{3,1,2,0:T(2,128)}, u32[]{:S(2)}) copy-start(f32[1,2,2,128]{3,1,2,0:T(2,128)} %copy-done.43) | copy-start | bytes 6148
  1996.1 141.5 %copy-start.27 = (bf16[512,768]{1,0:T(8,128)(2,1)S(1)}, bf16[512,768]{1,0:T(8,128)(2,1)}, u32[]{:S(2)}) copy-start(bf16[512,768]{1,0:T(8,128)(2,1)} %copy-done.26) | copy-start | bytes 2359300
  1996.1 141.5 %copy-start.42 = (s32[1,2,2,128]{3,1,2,0:T(2,128)S(1)}, s32[1,2,2,128]{3,1,2,0:T(2,128)}, u32[]{:S(2)}) copy-start(s32[1,2,2,128]{3,1,2,0:T(2,128)} %copy-done.41) | copy-start | bytes 6148
  1996.1 141.5 %copy-start.47 = (f32[512,2]{0,1:T(2,128)S(1)}, f32[512,2]{0,1:T(2,128)}, u32[]{:S(2)}) copy-start(f32[512,2]{0,1:T(2,128)} %copy-done.46) | copy-start | bytes 12292
  1996.1 141.5 %copy-start.49 = (f32[1,2,2,128]{3,1,2,0:T(2,128)S(1)}, f32[1,2,2,128]{3,1,2,0:T(2,128)}, u32[]{:S(2)}) copy-start(f32[1,2,2,128]{3,1,2,0:T(2,128)} %copy-done.48) | copy-start | bytes 6148
  1996.1 141.5 %copy-start.51 = (f32[512]{0:T(512)S(1)}, f32[512]{0:T(512)}, u32[]{:S(2)}) copy-start(f32[512]{0:T(512)} %copy-done.50) | copy-start | bytes 6148
  1996.1 141.9 %copy-start.40 = (f32[2,3,2047]{2,1,0:T(4,128)S(1)}, f32[2,3,2047]{2,1,0:T(4,128)}, u32[]{:S(2)}) copy-start(f32[2,3,2047]{2,1,0:T(4,128)} %get-tuple-element.569) | copy-start | bytes 147388
  1996.1 141.9 %copy-start.59 = (s32[2047]{0:T(1024)S(1)}, s32[2047]{0:T(1024)}, u32[]{:S(2)}) copy-start(s32[2047]{0:T(1024)} %param.29) | copy-start | bytes 24568
  1996.1 142.7 %copy-start.32 = (bf16[96,8,2,256]{3,1,2,0:T(8,128)(2,1)S(1)}, bf16[96,8,2,256]{3,1,2,0:T(8,128)(2,1)}, u32[]{:S(2)}) copy-start(bf16[96,8,2,256]{3,1,2,0:T(8,128)(2,1)} %copy-done.31) | copy-start | bytes 2359300
  1996.2 262.2 %all-reduce.7.cloned.1.call-start = ((), (), s32[]{:S(2)}) async-start(), calls=%async_computation.30 | async-start | bytes 5898240 | tf_op jit(solution)/shard_map/psum | solution.py:64
  2140.9 49.4 %copy-start.14 = (f32[512,768]{1,0:T(8,128)S(1)}, f32[512,768]{1,0:T(8,128)}, u32[]{:S(2)}) copy-start(f32[512,768]{1,0:T(8,128)} %copy-done.13) | copy-start | bytes 4718596
  2190.4 79.2 %copy-start.1 = (f32[32,12]{0,1:T(8,128)S(1)}, f32[32,12]{0,1:T(8,128)}, u32[]{:S(2)}) copy-start(f32[32,12]{0,1:T(8,128)} %param.28) | copy-start | bytes 4612
  (86 other events, 400.9 us)
Sparse Core Ops, SparseCore 0:
  9.9 26.7 all-gather.10
  38.6 24.0 all-gather.8
  64.6 24.0 all-gather.6
  90.4 24.0 all-gather.12
  115.9 37.4 all-gather.14
  154.8 37.4 all-gather.16
  904.5 42.6 reduce-scatter.12
  1903.7 39.7 reduce-scatter.10
  1947.5 42.4 reduce-scatter.8
  1994.1 42.4 reduce-scatter.6
  2039.2 47.8 reduce-scatter.16
  2089.6 47.8 reduce-scatter.14
  2140.9 117.4 all-reduce.6
where the time goes:
time: 2320 us; the launch traced here: 2280 us
  local copies, waits for them, and re-layouts  1310 us (56%)
  waiting for transfers between devices  344 us (15%)
  other arithmetic  250 us (11%)
  matrix products  164 us (7%)
  blocking collectives  99.7 us (4%)
  loops' own time  55.8 us (2%)
  starting transfers between devices  40.3 us (2%)
    rev x8, local copies, waits for them, and re-layouts, skew_bias(): return jnp.flip(shaped, axis=1)  388 us
    while x208, local copies, waits for them, and re-layouts  336 us
    rev x4, local copies, waits for them, and re-layouts, diagonal_sums(): flipped = jnp.flip(values, axis=1)  127 us
    reshape x8, local copies, waits for them, and re-layouts, skew_bias(): jnp.broadcast_to(values[:, None, :], (head_count, block, span))  107 us
    scatter-add x1, other arithmetic, local(): send_rows.at[token_ids, slot_safe]  75.6 us
    scatter-add x1, other arithmetic, local(): send_grads = jnp.zeros((experts, capacity, width), jnp.bfloat16).at[token...  75.5 us
    psum x1, waiting for transfers between devices, across_replicas(): lax.psum(query_part.astype(jnp.bfloat16), 'seq').astype(jnp.float32)  65 us
    reshape x4, local copies, waits for them, and re-layouts, diagonal_sums(): return jnp.sum(flat.reshape(head_count, block, span), axis=1)  62.7 us
  transfers between devices with their start and end apart: 23, of which 12 were waited for; matrix products, arithmetic and copies ran while one was open for 74% of the time, Pallas kernels for 0%

commit v1 on v0

v1 whole, which is shorter than its diff:
```python
import functools
import math

import jax
import jax.numpy as jnp
from jax import lax
from jax.experimental import pallas as pl
from jax.experimental.pallas import tpu as pltpu
from jax.sharding import PartitionSpec as P

eps = 1e-06
highest_precision = lax.Precision.HIGHEST
lanes = 128
vmem_limit = 56 * 1024 * 1024


def normalize(residual_stream, gain):
    factor = lax.rsqrt(jnp.mean(residual_stream * residual_stream, axis=-1, keepdims=True) + eps)
    return (residual_stream * factor * gain, factor)


def norm_back(grad_norm, residual_stream, factor, gain):
    gain_grad = jnp.sum(grad_norm * residual_stream * factor, axis=0)
    scaled = grad_norm * gain
    inner = jnp.mean(scaled * residual_stream, axis=-1, keepdims=True)
    return (scaled * factor - residual_stream * factor**3 * inner, gain_grad)


def dot_nt(left, right):
    return lax.dot_general(
        left, right, (((1,), (1,)), ((), ())), preferred_element_type=jnp.float32
    )


def dot_tn(left, right):
    return lax.dot_general(
        left, right, (((0,), (0,)), ((), ())), preferred_element_type=jnp.float32
    )


def dot_nn(left, right):
    return jnp.dot(left, right, preferred_element_type=jnp.float32)


def head_part(ref, start, width):
    part = ref[:, 0, :, start : start + width]
    return part.reshape(part.shape[0] * part.shape[1], width)


def attend_kernel(
    heads, head_width, rel_ref, rows_ref, seq_ref, out_ref, probs_ref, skew_ref, keys_ref, values_ref
):
    group = heads * head_width
    block = rows_ref.shape[2]
    length = keys_ref.shape[1]
    step = pl.program_id(1)

    @pl.when((pl.program_id(0) == 0) & (step == 0))
    def build_skew():
        for head in range(heads):
            spread = jnp.broadcast_to(rel_ref[head : head + 1, :], (lanes, 2 * length))
            skew_ref[head] = pltpu.roll(
                spread, 2 * length - (lanes - 1), 1, stride=1, stride_axis=0
            )

    @pl.when(step == 0)
    def split_heads():
        for head in range(heads):
            keys_ref[head] = head_part(seq_ref, group + head * head_width, head_width)
            values_ref[head] = head_part(seq_ref, 2 * group + head * head_width, head_width)

    mixed = []
    for head in range(heads):
        query = rows_ref[0, 0, :, head * head_width : (head + 1) * head_width]
        bias = []
        for sub in range(block // lanes):
            offset = length - lanes - step * block - sub * lanes
            bias.append(skew_ref[head, :, pl.ds(pl.multiple_of(offset, lanes), length)])
        scores = dot_nt(query, keys_ref[head]) * (1.0 / math.sqrt(head_width)) + jnp.concatenate(
            bias, axis=0
        )
        peak = jnp.max(scores, axis=-1, keepdims=True)
        weights = jnp.exp(scores - peak)
        inverse = 1.0 / jnp.sum(weights, axis=-1, keepdims=True)
        rounded = (weights * inverse).astype(jnp.bfloat16)
        probs_ref[0, head] = rounded
        mixed.append(dot_nn(rounded, values_ref[head]))
    out_ref[0, 0] = jnp.concatenate(mixed, axis=-1).astype(jnp.bfloat16)


def attend(rel_pad, qkv, heads, head_width):
    groups, seq_count, piece, triple = qkv.shape
    length = groups * piece
    group = heads * head_width
    pairs = seq_count * heads
    return pl.pallas_call(
        functools.partial(attend_kernel, heads, head_width),
        grid=(seq_count, groups),
        out_shape=(
            jax.ShapeDtypeStruct((groups, seq_count, piece, group), jnp.bfloat16),
            jax.ShapeDtypeStruct((seq_count, heads, length, length), jnp.bfloat16),
        ),
        in_specs=[
            pl.BlockSpec(rel_pad.shape, lambda s, i: (0, 0)),
            pl.BlockSpec((1, 1, piece, triple), lambda s, i: (i, s, 0, 0)),
            pl.BlockSpec((groups, 1, piece, triple), lambda s, i: (0, s, 0, 0)),
        ],
        out_specs=(
            pl.BlockSpec((1, 1, piece, group), lambda s, i: (i, s, 0, 0)),
            pl.BlockSpec((1, heads, piece, length), lambda s, i: (s, 0, i, 0)),
        ),
        scratch_shapes=[
            pltpu.VMEM((heads, lanes, 2 * length), jnp.float32),
            pltpu.VMEM((heads, length, head_width), jnp.bfloat16),
            pltpu.VMEM((heads, length, head_width), jnp.bfloat16),
        ],
        compiler_params=pltpu.CompilerParams(vmem_limit_bytes=vmem_limit),
        cost_estimate=pl.CostEstimate(
            flops=16 * pairs * length * length * head_width,
            bytes_accessed=2 * pairs * length * length,
            transcendentals=pairs * length * length,
        ),
    )(rel_pad, qkv, qkv)


def attend_back_kernel(
    heads,
    head_width,
    rows_ref,
    seq_ref,
    grad_ref,
    probs_ref,
    out_ref,
    rel_ref,
    keys_ref,
    values_ref,
    sums_ref,
    key_grad_ref,
    value_grad_ref,
):
    group = heads * head_width
    groups, _, block, _ = out_ref.shape
    length = keys_ref.shape[1]
    scale = 1.0 / math.sqrt(head_width)
    step = pl.program_id(1)

    @pl.when((pl.program_id(0) == 0) & (step == 0))
    def clear_sums():
        sums_ref[...] = jnp.zeros_like(sums_ref)

    @pl.when(step == 0)
    def split_heads():
        key_grad_ref[...] = jnp.zeros_like(key_grad_ref)
        value_grad_ref[...] = jnp.zeros_like(value_grad_ref)
        for head in range(heads):
            keys_ref[head] = head_part(seq_ref, group + head * head_width, head_width)
            values_ref[head] = head_part(seq_ref, 2 * group + head * head_width, head_width)

    query_turned = rows_ref[0, 0, :, :group].T
    grad_turned = grad_ref[0, 0].T
    query_grads = []
    for head in range(heads):
        span = slice(head * head_width, (head + 1) * head_width)
        grad = grad_ref[0, 0, :, span]
        rounded = probs_ref[0, head]
        weights = rounded.astype(jnp.float32)
        weight_grad = dot_nt(grad, values_ref[head])
        product = weights * weight_grad
        inner = jnp.sum(product, axis=-1, keepdims=True)
        score_grad = product - weights * inner
        score_low = score_grad.astype(jnp.bfloat16)
        for sub in range(block // lanes):
            offset = length - lanes - step * block - sub * lanes
            place = pl.ds(pl.multiple_of(offset, lanes), length)
            sums_ref[head, :, place] += score_grad[sub * lanes : (sub + 1) * lanes]
        query_grads.append(dot_nn(score_low, keys_ref[head]) * scale)
        key_grad_ref[span] += dot_nn(query_turned[span], score_low)
        value_grad_ref[span] += dot_nn(grad_turned[span], rounded)
    out_ref[step, 0, :, :group] = jnp.concatenate(query_grads, axis=-1).astype(jnp.bfloat16)

    @pl.when(step == groups - 1)
    def store_sums():
        key_grad = (key_grad_ref[...] * scale).T.astype(jnp.bfloat16)
        value_grad = value_grad_ref[...].T.astype(jnp.bfloat16)
        out_ref[:, 0, :, group : 2 * group] = key_grad.reshape(groups, block, group)
        out_ref[:, 0, :, 2 * group :] = value_grad.reshape(groups, block, group)

    @pl.when((pl.program_id(0) == pl.num_programs(0) - 1) & (step == groups - 1))
    def fold_sums():
        for head in range(heads):
            folded = sums_ref[head]
            while folded.shape[0] > 1:
                half = folded.shape[0] // 2
                folded = folded[half:] + pltpu.roll(folded[:half], half, 1)
            rel_ref[head : head + 1, :] = folded


def attend_back(qkv, grads, probs, heads, head_width):
    groups, seq_count, piece, triple = qkv.shape
    length = groups * piece
    group = heads * head_width
    pairs = seq_count * heads
    return pl.pallas_call(
        functools.partial(attend_back_kernel, heads, head_width),
        grid=(seq_count, groups),
        out_shape=(
            jax.ShapeDtypeStruct(qkv.shape, jnp.bfloat16),
            jax.ShapeDtypeStruct((heads, 2 * length), jnp.float32),
        ),
        in_specs=[
            pl.BlockSpec((1, 1, piece, triple), lambda s, i: (i, s, 0, 0)),
            pl.BlockSpec((groups, 1, piece, triple), lambda s, i: (0, s, 0, 0)),
            pl.BlockSpec((1, 1, piece, group), lambda s, i: (i, s, 0, 0)),
            pl.BlockSpec((1, heads, piece, length), lambda s, i: (s, 0, i, 0)),
        ],
        out_specs=(
            pl.BlockSpec((groups, 1, piece, triple), lambda s, i: (0, s, 0, 0)),
            pl.BlockSpec((heads, 2 * length), lambda s, i: (0, 0)),
        ),
        scratch_shapes=[
            pltpu.VMEM((heads, length, head_width), jnp.bfloat16),
            pltpu.VMEM((heads, length, head_width), jnp.bfloat16),
            pltpu.VMEM((heads, lanes, 2 * length), jnp.float32),
            pltpu.VMEM((group, length), jnp.float32),
            pltpu.VMEM((group, length), jnp.float32),
        ],
        compiler_params=pltpu.CompilerParams(vmem_limit_bytes=vmem_limit),
        cost_estimate=pl.CostEstimate(
            flops=32 * pairs * length * length * head_width,
            bytes_accessed=2 * pairs * length * length,
            transcendentals=0,
        ),
    )(qkv, qkv, grads, probs)


def expert_kernel(
    width, both_ref, first_ref, second_ref, back_ref, first_grad_ref, second_grad_ref, turned_ref, sum_ref
):
    step = pl.program_id(0)

    @pl.when(step == 0)
    def start_sums():
        sum_ref[...] = jnp.zeros_like(sum_ref)
        turned_ref[...] = both_ref[:, :width].T

    rows = both_ref[:, :width]
    grads = both_ref[:, width:]
    first = first_ref[...]
    second = second_ref[...]
    hidden = dot_nn(rows, first)
    chance = 0.5 + 0.5 * lax.erf(hidden * math.sqrt(0.5))
    active = (hidden * chance).astype(jnp.bfloat16)
    density = jnp.exp(hidden * hidden * -0.5) * (1.0 / math.sqrt(2.0 * math.pi))
    slope = chance + hidden * density
    hidden_grad = (dot_nt(grads, second) * slope).astype(jnp.bfloat16)
    sum_ref[:, :width] += dot_nn(active, second)
    sum_ref[:, width:] += dot_nt(hidden_grad, first)
    second_grad_ref[...] = dot_tn(active, grads).astype(jnp.bfloat16)
    first_grad_ref[...] = dot_nn(turned_ref[...], hidden_grad).astype(jnp.bfloat16)

    @pl.when(step == pl.num_programs(0) - 1)
    def store_sums():
        back_ref[...] = sum_ref[...].astype(jnp.bfloat16)


def expert_layer(both, first, second):
    rows, double = both.shape
    width, hidden_width = first.shape
    block = 512 if hidden_width % 512 == 0 else hidden_width
    return pl.pallas_call(
        functools.partial(expert_kernel, width),
        grid=(hidden_width // block,),
        out_shape=(
            jax.ShapeDtypeStruct(both.shape, jnp.bfloat16),
            jax.ShapeDtypeStruct(first.shape, jnp.bfloat16),
            jax.ShapeDtypeStruct(second.shape, jnp.bfloat16),
        ),
        in_specs=[
            pl.BlockSpec(both.shape, lambda f: (0, 0)),
            pl.BlockSpec((width, block), lambda f: (0, f)),
            pl.BlockSpec((block, width), lambda f: (f, 0)),
        ],
        out_specs=(
            pl.BlockSpec(both.shape, lambda f: (0, 0)),
            pl.BlockSpec((width, block), lambda f: (0, f)),
            pl.BlockSpec((block, width), lambda f: (f, 0)),
        ),
        scratch_shapes=[
            pltpu.VMEM((width, rows), jnp.bfloat16),
            pltpu.VMEM(both.shape, jnp.float32),
        ],
        compiler_params=pltpu.CompilerParams(vmem_limit_bytes=vmem_limit),
        cost_estimate=pl.CostEstimate(
            flops=12 * rows * width * hidden_width,
            bytes_accessed=8 * width * hidden_width,
            transcendentals=2 * rows * hidden_width,
        ),
    )(both, first, second)


def exchange(values, axis):
    return lax.all_to_all(values, axis, split_axis=0, concat_axis=0, tiled=True)


def local(
    tokens,
    attn_gain,
    w_query,
    w_key,
    w_value,
    output_projection_weight,
    bias_table,
    rel_buckets,
    ffn_gain,
    router,
    expert_in,
    expert_out,
    expert_ids,
    cotangent,
):
    seq_count, piece, width = tokens.shape
    groups = lax.axis_size("seq")
    length = piece * groups
    rows = seq_count * piece
    bucket_count, heads_all = bias_table.shape
    local_heads = heads_all // groups
    head_width = width // heads_all
    group_width = local_heads * head_width
    triple = 3 * group_width
    experts = router.shape[1]
    capacity = (5 * rows + 4 * experts - 1) // (4 * experts)
    low = jnp.bfloat16
    high = jnp.float32
    shard_rows = w_query.shape[0]

    def by_group(weight):
        return weight.reshape(shard_rows, groups, group_width).transpose(1, 0, 2)

    projections = jnp.concatenate([by_group(w_query), by_group(w_key), by_group(w_value)], axis=-1)
    full_qkv = lax.all_gather(projections, ("dp", "expert"), axis=1, tiled=True)
    full_output = lax.all_gather(output_projection_weight, ("dp", "expert"), axis=0, tiled=True)
    first_weight = lax.all_gather(expert_in, "dp", axis=1, tiled=True)[0]
    second_weight = lax.all_gather(expert_out, "dp", axis=1, tiled=True)[0]
    output_groups = full_output.reshape(groups, group_width, width)

    residual_stream = tokens.reshape(rows, width).astype(high)
    normed_one, factor_one = normalize(residual_stream, attn_gain)
    first_layer_norm = normed_one.astype(low)
    qkv_rows = jnp.einsum(
        "rm,gmc->grc", first_layer_norm, full_qkv, preferred_element_type=high
    ).astype(low)
    qkv = exchange(qkv_rows.reshape(groups, seq_count, piece, triple), "seq")

    head_start = lax.axis_index("seq") * local_heads
    table_part = lax.dynamic_slice_in_dim(bias_table, head_start, local_heads, 1)
    bucket_onehot = (rel_buckets[:, None] == jnp.arange(bucket_count)[None, :]).astype(high)
    bucket_onehot = jnp.pad(bucket_onehot, ((0, 1), (0, 0)))
    rel_pad = jnp.dot(table_part.T, bucket_onehot.T, precision=highest_precision)
    mixed, probs_kept = attend(rel_pad, qkv, local_heads, head_width)
    attended = exchange(mixed, "seq").reshape(groups, rows, group_width)
    second_branch = residual_stream + jnp.einsum(
        "grc,gcm->rm", attended, output_groups, preferred_element_type=high
    )
    normed_two, factor_two = normalize(second_branch, ffn_gain)
    second_layer_norm = normed_two.astype(low)
    router_logits = jnp.dot(second_layer_norm, router, preferred_element_type=high)
    probs = jax.nn.softmax(router_logits, axis=-1)
    token_ids = expert_ids.reshape(rows)
    onehot = token_ids[:, None] == jnp.arange(experts)[None, :]
    onehot_float = onehot.astype(high)
    gate = jnp.sum(probs * onehot_float, axis=-1)
    earlier = (jnp.arange(rows)[:, None] > jnp.arange(rows)[None, :]).astype(low)
    ranks = jnp.dot(earlier, onehot.astype(low), preferred_element_type=high)
    slots = jnp.sum(ranks * onehot_float, axis=-1).astype(jnp.int32)
    kept = slots < capacity
    keep = kept.astype(high)
    target = jnp.where(kept, token_ids * capacity + slots, -1)
    dispatch = (target[:, None] == jnp.arange(experts * capacity)[None, :]).astype(low)
    out_grad = cotangent.reshape(rows, width).astype(high)
    result_grad = (gate[:, None] * out_grad * keep[:, None]).astype(low)
    outgoing = jnp.concatenate([second_layer_norm, result_grad], axis=-1)
    send = dot_tn(dispatch, outgoing).astype(low)
    received = exchange(send.reshape(experts, capacity, 2 * width), "expert")
    back, first_grad, second_grad = expert_layer(
        received.reshape(experts * capacity, 2 * width), first_weight, second_weight
    )
    returned = exchange(back.reshape(experts, capacity, 2 * width), "expert")
    per_token = dot_nn(dispatch, returned.reshape(experts * capacity, 2 * width))
    token_result = per_token[:, :width]
    layer_out = (second_branch + gate[:, None] * token_result).astype(low)
    gate_grad = jnp.sum(out_grad * token_result, axis=-1)
    logit_grad = probs * (onehot_float * gate_grad[:, None] - (gate * gate_grad)[:, None])
    router_grad = jnp.dot(
        second_layer_norm.astype(high).T, logit_grad, precision=highest_precision
    )
    norm_two_grad = jnp.dot(logit_grad, router.astype(high).T, precision=highest_precision)
    norm_two_grad = norm_two_grad + per_token[:, width:]
    second_back, ffn_gain_grad = norm_back(norm_two_grad, second_branch, factor_two, ffn_gain)
    second_grad_total = out_grad + second_back
    grad_low = second_grad_total.astype(low)
    attended_grad = jnp.einsum(
        "rm,gcm->grc", grad_low, output_groups, preferred_element_type=high
    ).astype(low)
    heads_grad = exchange(attended_grad.reshape(groups, seq_count, piece, group_width), "seq")
    output_weight_grad = jnp.einsum("grc,rm->gcm", attended, grad_low, preferred_element_type=high)
    qkv_back, rel_back = attend_back(qkv, heads_grad, probs_kept, local_heads, head_width)
    table_local = jnp.dot(bucket_onehot.T, rel_back.T, precision=highest_precision)
    table_grad = lax.dynamic_update_slice_in_dim(
        jnp.zeros((bucket_count, heads_all), high), table_local, head_start, 1
    )
    qkv_tok = exchange(qkv_back, "seq").reshape(groups, rows, triple)
    qkv_weight_grad = jnp.einsum(
        "rm,grc->mgc", first_layer_norm, qkv_tok, preferred_element_type=high
    ).astype(low)
    norm_one_grad = jnp.einsum("grc,gmc->rm", qkv_tok, full_qkv, preferred_element_type=high)
    first_back, attn_gain_grad = norm_back(norm_one_grad, residual_stream, factor_one, attn_gain)
    input_grad = second_grad_total + first_back

    first_share = lax.psum(
        lax.psum_scatter(first_grad, "dp", scatter_dimension=0, tiled=True), "seq"
    )
    second_share = lax.psum(
        lax.psum_scatter(second_grad, "dp", scatter_dimension=0, tiled=True), "seq"
    )
    output_share = lax.psum(
        lax.psum_scatter(
            output_weight_grad.reshape(width, width).astype(low),
            ("dp", "expert"),
            scatter_dimension=0,
            tiled=True,
        ),
        "seq",
    )
    qkv_share = lax.psum(
        lax.psum_scatter(
            qkv_weight_grad.reshape(width, groups * triple),
            ("dp", "expert"),
            scatter_dimension=0,
            tiled=True,
        ),
        "seq",
    )
    qkv_share = qkv_share.astype(high).reshape(shard_rows, groups, triple)

    def from_group(part):
        return (
            qkv_share[:, :, part * group_width : (part + 1) * group_width]
            .reshape(shard_rows, width)
        )

    attn_gain_total, ffn_gain_total, router_total, table_total = lax.psum(
        (attn_gain_grad, ffn_gain_grad, router_grad, table_grad), ("dp", "expert", "seq")
    )
    return (
        layer_out.reshape(seq_count, piece, width),
        input_grad.reshape(seq_count, piece, width),
        attn_gain_total,
        from_group(0),
        from_group(1),
        from_group(2),
        output_share.astype(high),
        table_total,
        ffn_gain_total,
        router_total,
        first_share.astype(high)[None],
        second_share.astype(high)[None],
    )


def solution(mesh):
    placed = (
        P(("dp", "expert"), "seq", None),
        P(),
        P(("dp", "expert"), None),
        P(("dp", "expert"), None),
        P(("dp", "expert"), None),
        P(("dp", "expert"), None),
        P(),
        P(),
        P(),
        P(),
        P("expert", "dp", None),
        P("expert", "dp", None),
        P(("dp", "expert"), "seq"),
        P(("dp", "expert"), "seq", None),
    )
    return jax.shard_map(
        local,
        mesh=mesh,
        in_specs=placed,
        out_specs=(
            P(("dp", "expert"), "seq", None),
            P(("dp", "expert"), "seq", None),
            P(),
            P(("dp", "expert"), None),
            P(("dp", "expert"), None),
            P(("dp", "expert"), None),
            P(("dp", "expert"), None),
            P(),
            P(),
            P(),
            P("expert", "dp", None),
            P("expert", "dp", None),
        ),
        check_vma=False,
    )
```

time: 2320 us -> 703 us (0.30); the launches traced: 2280 us -> 702 us
  local copies, waits for them, and re-layouts: 1310 us -> 31.9 us
  other arithmetic: 250 us -> 12.4 us
  matrix products: 164 us -> 25 us
  Pallas kernels: 0 us -> 73.8 us
  loops' own time: 55.8 us -> 0 us
  blocking collectives: 99.7 us -> 146 us
  waiting for transfers between devices: 344 us -> 384 us
  starting transfers between devices: 40.3 us -> 13.6 us
    rev x12 -> x0, local copies, waits for them, and re-layouts: 515 us -> none  [the longest x8 388 us: skew_bias(): return jnp.flip(shaped, axis=1)]
    while x214 -> x0, local copies, waits for them, and re-layouts: 344 us -> none
    reshape x30 -> x11, local copies, waits for them, and re-layouts: 193 us -> 9.63 us  [the longest x4 3.34 us: by_group(): return weight.reshape(shard_rows, groups, group_width).transpose(1, 0, 2)]
    scatter-add x2 -> x0, other arithmetic: 151 us -> none  [the longest x1 75.6 us: local(): send_rows.at[token_ids, slot_safe]]
    dot_general x52 -> x13, matrix products: 164 us -> 23.8 us  [the longest x1 4.52 us: local(): jnp.einsum('rm,gmc->grc', first_layer_norm, full_qkv, preferred_element_t...]
    slice x13 -> x1, local copies, waits for them, and re-layouts: 76.9 us -> 0.1 us  [from_group(): qkv_share[:, :, part * group_width:(part + 1) * group_width]]
    pallas_call x0 -> x3, Pallas kernels: none -> 73.8 us  [the longest x1 26.7 us: attend_back(): pl.pallas_call(functools.partial(attend_back_kernel, heads, head_width),...]
    another operation x6 -> x0, loops' own time: 55.8 us -> none  [the longest x1 30.7 us: local(): lax.map(backward_sequence, (heads_query, heads_key, heads_value, heads_gr...]
  transfers between devices with their start and end apart: 23 -> 12, of which waited for: 12 -> 9; matrix products, arithmetic and copies ran while one was open for 74% -> 5% of each run, Pallas kernels for 0% -> 3%
where the time goes in v1:
time: 703 us; the launch traced here: 702 us
  waiting for transfers between devices  384 us (55%)
  blocking collectives  146 us (21%)
  Pallas kernels  73.8 us (10%)
  local copies, waits for them, and re-layouts  31.9 us (5%)
  matrix products  25 us (4%)
  between operations  14.3 us (2%)
  starting transfers between devices  13.6 us (2%)
  other arithmetic  12.4 us (2%)
    all_to_all x3, blocking collectives, exchange(): return lax.all_to_all(values, axis, split_axis=0, concat_axis=0, tiled=True)  102 us
    all_to_all x3, waiting for transfers between devices, exchange(): return lax.all_to_all(values, axis, split_axis=0, concat_axis=0, tiled=True)  94.2 us
    psum x1, waiting for transfers between devices, local(): lax.psum(lax.psum_scatter(qkv_weight_grad.reshape(width, groups * triple)...  69.2 us
    reduce_scatter x1, waiting for transfers between devices, local(): lax.psum_scatter(first_grad, 'dp', scatter_dimension=0, tiled=True)  50.6 us
    reduce_scatter x1, waiting for transfers between devices, local(): lax.psum_scatter(second_grad, 'dp', scatter_dimension=0, tiled=True)  50.4 us
    unnamed x10, waiting for transfers between devices  45.3 us
    psum x1, blocking collectives, local(): lax.psum((attn_gain_grad, ffn_gain_grad, router_grad, table_grad), ('dp',...  44.6 us
    reduce_scatter x1, waiting for transfers between devices, local(): lax.psum_scatter(output_weight_grad.reshape(width, width).astype(low), ('...  38.4 us
  transfers between devices with their start and end apart: 12, of which 9 were waited for; matrix products, arithmetic and copies ran while one was open for 5% of the time, Pallas kernels for 3%

profile of v1, /device:TPU:0, one launch (start us, length us, event | category | flops | bytes accessed | tf_op | source)
XLA Modules:
  0.0 701.8 jit_solution(6181082912009841548)
XLA Ops:
  7.2 1.1 reshape.178
  8.4 1.1 reshape.179
  9.5 1.1 reshape.177
  10.7 0.9 pad_maximum_fusion
  11.7 0.7 all-gather.7.cloned.1.call-update
  12.4 0.7 all-gather.9.cloned.1.call-update
  13.7 36.5 %all-gather.5.cloned.1.call-done = bf16[4,768,576]{2,1,0:T(8,128)(2,1)} async-done(((bf16[4,96,576]{2,1,0:T(8,128)(2,1)}), bf16[4,768,576]{2,1,0:T(8,128)(2,1)}) %all-gather.5.cloned.1.call-update) | async-done | bytes 3538960 | tf_op jit(solution)/shard_map/all_gather | solution.py:340
  50.1 4.5 convolution_convert_fusion.1
  54.6 1.6 copy.76
  56.2 4.7 all-to-all-start
  60.9 0.6 all-gather.11.cloned.1.call-update
  61.5 0.3 iota_compare_fusion.4
  61.8 1.2 fusion.19.rel_ref
  63.0 52.1 %all-to-all-done = bf16[4,2,256,576]{2,3,1,0:T(8,128)(2,1)S(1)} async-done(((bf16[4,2,256,576]{2,3,1,0:T(8,128)(2,1)}), bf16[4,2,256,576]{2,3,1,0:T(8,128)(2,1)S(1)}, u32[]{:S(2)}, u32[]{:S(2)}) %all-to-all-start) | async-done | bytes 2359328 | tf_op jit(solution)/shard_map/all_to_all | solution.py:302
  115.2 2.6 copy.46.rows_ref.seq_ref
  117.7 21.3 %shard_map.229 = (bf16[4,2,256,192]{3,2,1,0:T(8,128)(2,1)}, bf16[2,3,1024,1024]{3,2,1,0:T(8,128)(2,1)}) custom-call(f32[3,2048]{1,0:T(4,128)} %fusion.19.rel_ref, bf16[4,2,256,576]{3,2,1,0:T(8,128)(2,1)} %copy.46.rows_ref.seq_ref, bf16[4,2,256,576]{3,2,1,0:T(8,128)(2,1)} %copy.46.rows_ref.seq_ref), custom_call_target="tpu_custom_call" | custom-call | flops 6442450944 | bytes 12582912 | tf_op jit(solution)/shard_map/pallas_call | solution.py:96
  139.0 2.2 copy.48
  141.3 3.6 all-to-all-start.1
  145.2 19.4 %all-to-all-done.1 = bf16[4,2,256,192]{2,3,1,0:T(8,128)(2,1)S(1)} async-done(((bf16[4,2,256,192]{2,3,1,0:T(8,128)(2,1)}), bf16[4,2,256,192]{2,3,1,0:T(8,128)(2,1)S(1)}, u32[]{:S(2)}, u32[]{:S(2)}) %all-to-all-start.1) | async-done | bytes 786464 | tf_op jit(solution)/shard_map/all_to_all | solution.py:302
  164.7 2.5 multiply_reduce_fusion.2
  167.4 0.4 copy-done.18
  167.8 0.3 fusion.46
  168.6 2.6 convolution_convert_fusion
  171.2 4.8 all-to-all-start.2
  176.3 22.7 %all-to-all-done.2 = bf16[2,320,1536]{2,1,0:T(8,128)(2,1)} async-done(((bf16[2,320,1536]{2,1,0:T(8,128)(2,1)}), bf16[2,320,1536]{2,1,0:T(8,128)(2,1)}, u32[]{:S(2)}, u32[]{:S(2)}) %all-to-all-start.2) | async-done | bytes 1966112 | tf_op jit(solution)/shard_map/all_to_all | solution.py:302
  199.0 25.8 %shard_map.230 = (bf16[640,1536]{1,0:T(8,128)(2,1)}, bf16[768,3072]{1,0:T(8,128)(2,1)}, bf16[3072,768]{1,0:T(8,128)(2,1)}) custom-call(bf16[640,1536]{1,0:T(8,128)(2,1)} %bitcast.10.both_ref, bf16[768,3072]{1,0:T(8,128)(2,1)} %bitcast.141, bf16[3072,768]{1,0:T(8,128)(2,1)} %bitcast.142), custom_call_target="tpu_custom_call" | custom-call | flops 18119393280 | bytes 18874368 | tf_op jit(solution)/shard_map/pallas_call | solution.py:270
  224.8 25.7 %all_to_all.30 = bf16[2,320,1536]{2,1,0:T(8,128)(2,1)S(1)} all-to-all(bf16[2,320,1536]{2,1,0:T(8,128)(2,1)} %bitcast.120), channel_id=1, replica_groups=mesh['dp'=4,'expert'=2,'seq'=4] {'expert'}, dimensions={0} | all-to-all | bytes 3932160 | tf_op jit(solution)/shard_map/all_to_all | solution.py:302
  250.5 1.4 fusion.17
  252.0 1.3 fusion.2
  253.3 1.2 multiply_reduce_fusion
  254.5 0.4 convert_add_fusion
  255.0 0.8 copy-done.22
  255.8 0.8 convolution_convert_fusion.3
  256.7 20.2 %all_to_all.31 = bf16[4,2,256,192]{2,3,1,0:T(8,128)(2,1)S(1)} all-to-all(bf16[4,2,256,192]{2,3,1,0:T(8,128)(2,1)S(1)} %bitcast.115), channel_id=1, replica_groups=mesh['dp'=4,'expert'=2,'seq'=4] {'seq'}, dimensions={0} | all-to-all | bytes 1572864 | tf_op jit(solution)/shard_map/all_to_all | solution.py:302
  276.8 1.3 copy.53.grad_ref
  278.1 26.7 %shard_map.231 = (bf16[4,2,256,576]{3,2,1,0:T(8,128)(2,1)}, f32[3,2048]{1,0:T(4,128)}) custom-call(bf16[4,2,256,576]{3,2,1,0:T(8,128)(2,1)} %copy.46.rows_ref.seq_ref, bf16[4,2,256,576]{3,2,1,0:T(8,128)(2,1)} %copy.46.rows_ref.seq_ref, bf16[4,2,256,192]{3,2,1,0:T(8,128)(2,1)} %copy.53.grad_ref, bf16[2,3,1024,1024]{3,2,1,0:T(8,128)(2,1)} %get-tuple-element.21.probs_ref), custom_call_target="tpu_custom_call" | custom-call | flops 12884901888 | bytes 12582912 | tf_op jit(solution)/shard_map/pallas_call | solution.py:203
  304.8 4.3 copy.54
  309.2 55.9 %all_to_all.32 = bf16[4,2,256,576]{2,3,1,0:T(8,128)(2,1)S(1)} all-to-all(bf16[4,2,256,576]{2,3,1,0:T(8,128)(2,1)} %copy.54), channel_id=1, replica_groups=mesh['dp'=4,'expert'=2,'seq'=4] {'seq'}, dimensions={0} | all-to-all | bytes 4718592 | tf_op jit(solution)/shard_map/all_to_all | solution.py:302
  365.1 3.9 bitcast_convert_fusion
  369.0 5.8 copy.63
  374.9 1.1 copy-done.11
  376.0 1.8 convolution_convert_fusion.2
  377.8 0.7 reduce-scatter.9.cloned.1.call-update
  378.6 0.7 reduce-scatter.11.cloned.1.call-update
  379.3 41.9 %reduce-scatter.13.cloned.1.call-done = bf16[96,2304]{1,0:T(8,128)(2,1)} async-done(((bf16[768,2304]{1,0:T(8,128)(2,1)}), bf16[96,2304]{1,0:T(8,128)(2,1)}) %reduce-scatter.13.cloned.1.call-update) | async-done | bytes 442384
  421.2 2.1 copy.64
  423.3 38.4 %reduce-scatter.7.cloned.1.call-done = bf16[96,768]{1,0:T(8,128)(2,1)} async-done(((bf16[768,768]{1,0:T(8,128)(2,1)}), bf16[96,768]{1,0:T(8,128)(2,1)}) %reduce-scatter.7.cloned.1.call-update) | async-done | bytes 147472 | tf_op jit(solution)/shard_map/reduce_scatter | solution.py:426
  461.7 50.6 %reduce-scatter.9.cloned.1.call-done = bf16[192,3072]{1,0:T(8,128)(2,1)} async-done(((bf16[768,3072]{1,0:T(8,128)(2,1)}), bf16[192,3072]{1,0:T(8,128)(2,1)}) %reduce-scatter.9.cloned.1.call-update) | async-done | bytes 1179664 | tf_op jit(solution)/shard_map/reduce_scatter | solution.py:420
  512.3 50.4 %reduce-scatter.11.cloned.1.call-done = bf16[768,768]{1,0:T(8,128)(2,1)} async-done(((bf16[3072,768]{1,0:T(8,128)(2,1)}), bf16[768,768]{1,0:T(8,128)(2,1)}) %reduce-scatter.11.cloned.1.call-update) | async-done | bytes 1179664 | tf_op jit(solution)/shard_map/reduce_scatter | solution.py:423
  562.7 0.4 fusion.43
  563.1 0.3 copy-done.16
  563.4 0.4 fusion.21
  564.0 2.0 copy.68
  566.0 0.8 copy-done.21
  566.8 3.6 fusion.7
  570.4 44.6 %all-reduce.1 = (f32[768]{0:T(1024)}, f32[32,12]{0,1:T(8,128)}, f32[768]{0:T(1024)}, f32[768,2]{0,1:T(2,128)}) all-reduce(f32[768]{0:T(1024)S(1)} %get-tuple-element.28, f32[32,12]{0,1:T(8,128)S(1)} %dynamic_update_slice.3, f32[768]{0:T(1024)S(1)} %get-tuple-element.26, ...), channel_id=1, replica_groups=mesh['dp'=4,'expert'=2,'seq'=4] {'dp','expert','seq'}, use_global_device_ids=true, to_apply=%region_10.11 | all-reduce | flops 3456 | bytes 27648 | tf_op jit(solution)/shard_map/psum | solution.py:451
  615.0 3.0 fusion.15
  618.0 69.2 %all-reduce.5.cloned.1.call-done = (bf16[96,4,576]{0,2,1:T(8,128)(2,1)}, bf16[96,768]{1,0:T(8,128)(2,1)}, bf16[1,192,3072]{2,1,0:T(8,128)(2,1)}, bf16[1,768,768]{2,1,0:T(8,128)(2,1)}) async-done(((bf16[96,4,576]{0,2,1:T(8,128)(2,1)}, bf16[96,768]{1,0:T(8,128)(2,1)}, bf16[1,192,3072]{2,1,0:T(8,128)(2,1)}, bf16[1,768,768]{2,1,0:T(8,128)(2,1)}), (bf16[96,4,576]{0,2,1:T(8,128)(2,1)}, bf16[96,768]{1,0:T(8,128)(2,1)}, ...) | async-done | bytes 2949136 | tf_op jit(solution)/shard_map/psum | solution.py:434
  687.2 3.0 broadcast_in_dim.19
  690.2 1.6 broadcast_in_dim.21
  691.9 0.9 copy.60
  692.8 0.9 copy.61
  693.7 0.9 copy.62
  694.5 0.7 convert_element_type.107
  (81 shorter events, 2.5 us)
Async XLA Ops:
  7.2 54.7 %copy-start = (f32[32,12]{0,1:T(8,128)S(1)}, f32[32,12]{0,1:T(8,128)}, u32[]{:S(2)}) copy-start(f32[32,12]{0,1:T(8,128)} %param.20) | copy-start | bytes 4612
  7.2 42.9 %all-gather.5.cloned.1.call-start = ((), (), s32[]{:S(2)}) async-start(), calls=%async_computation.10 | async-start | bytes 4423680 | tf_op jit(solution)/shard_map/all_gather | solution.py:340
  10.7 2.5 copy-start.3
  11.6 1.8 copy-start.17
  11.6 153.0 %all-gather.7.cloned.1.call-start = ((), (), s32[]{:S(2)}) async-start(), calls=%async_computation.11 | async-start | bytes 1327104 | tf_op jit(solution)/shard_map/all_gather | solution.py:341
  12.4 163.8 %all-gather.9.cloned.1.call-start = ((), (), s32[]{:S(2)}) async-start(), calls=%async_computation.12 | async-start | bytes 5898240 | tf_op jit(solution)/shard_map/all_gather | solution.py:342
  56.2 5.3 copy-start.19
  56.2 59.0 %all-to-all-start = ((bf16[4,2,256,576]{2,3,1,0:T(8,128)(2,1)}), bf16[4,2,256,576]{2,3,1,0:T(8,128)(2,1)S(1)}, u32[]{:S(2)}, u32[]{:S(2)}) async-start(bf16[4,2,256,576]{2,3,1,0:T(8,128)(2,1)} %bitcast.110), calls=%async_computation | async-start | bytes 4718592 | tf_op jit(solution)/shard_map/all_to_all | solution.py:302
  60.9 115.3 %all-gather.11.cloned.1.call-start = ((), (), s32[]{:S(2)}) async-start(), calls=%async_computation.13 | async-start | bytes 5898240 | tf_op jit(solution)/shard_map/all_gather | solution.py:343
  139.0 5.9 copy-start.20
  141.2 23.4 %copy-start.4 = (bf16[2,256,768]{2,1,0:T(8,128)(2,1)S(1)}, bf16[2,256,768]{2,1,0:T(8,128)(2,1)}, u32[]{:S(2)}) copy-start(bf16[2,256,768]{2,1,0:T(8,128)(2,1)} %param.14) | copy-start | bytes 2359300
  141.3 23.3 %all-to-all-start.1 = ((bf16[4,2,256,192]{2,3,1,0:T(8,128)(2,1)}), bf16[4,2,256,192]{2,3,1,0:T(8,128)(2,1)S(1)}, u32[]{:S(2)}, u32[]{:S(2)}) async-start(bf16[4,2,256,192]{2,3,1,0:T(8,128)(2,1)} %copy.48), calls=%async_computation.1 | async-start | bytes 1572864 | tf_op jit(solution)/shard_map/all_to_all | solution.py:302
  164.6 2.5 copy-start.10
  164.7 2.5 copy-start.15
  167.1 0.7 copy-start.18
  167.2 1.1 copy-start.8
  167.8 3.4 copy-start.6
  171.2 27.8 %all-to-all-start.2 = ((bf16[2,320,1536]{2,1,0:T(8,128)(2,1)}), bf16[2,320,1536]{2,1,0:T(8,128)(2,1)}, u32[]{:S(2)}, u32[]{:S(2)}) async-start(bf16[2,320,1536]{2,1,0:T(8,128)(2,1)} %bitcast.119), calls=%async_computation.2 | async-start | bytes 3932160 | tf_op jit(solution)/shard_map/all_to_all | solution.py:302
  176.0 245.3 %reduce-scatter.13.cloned.1.call-start = ((), (), s32[]{:S(2)}) async-start(), calls=%async_computation.17 | async-start | bytes 3981312
  253.3 1.2 copy-start.9
  254.5 1.3 copy-start.22
  309.2 55.9 %copy-start.5 = (bf16[2,256,768]{2,1,0:T(8,128)(2,1)S(1)}, bf16[2,256,768]{2,1,0:T(8,128)(2,1)}, u32[]{:S(2)}) copy-start(bf16[2,256,768]{2,1,0:T(8,128)(2,1)} %param.14) | copy-start | bytes 2359300
  365.1 3.9 copy-start.2
  374.8 1.1 copy-start.11
  374.8 86.8 %reduce-scatter.7.cloned.1.call-start = ((), (), s32[]{:S(2)}) async-start(), calls=%async_computation.14 | async-start | bytes 1327104 | tf_op jit(solution)/shard_map/reduce_scatter | solution.py:426
  377.8 134.5 %reduce-scatter.9.cloned.1.call-start = ((), (), s32[]{:S(2)}) async-start(), calls=%async_computation.15 | async-start | bytes 5898240 | tf_op jit(solution)/shard_map/reduce_scatter | solution.py:420
  378.5 184.1 %reduce-scatter.11.cloned.1.call-start = ((), (), s32[]{:S(2)}) async-start(), calls=%async_computation.16 | async-start | bytes 5898240 | tf_op jit(solution)/shard_map/reduce_scatter | solution.py:423
  379.3 307.9 %all-reduce.5.cloned.1.call-start = ((), (), s32[]{:S(2)}) async-start(), calls=%async_computation.18 | async-start | bytes 6193152 | tf_op jit(solution)/shard_map/psum | solution.py:434
  423.3 139.4 %copy-start.7 = (bf16[512,768]{1,0:T(8,128)(2,1)S(1)}, bf16[512,768]{1,0:T(8,128)(2,1)}, u32[]{:S(2)}) copy-start(bf16[512,768]{1,0:T(8,128)(2,1)} %copy-done.6) | copy-start | bytes 2359300
  562.7 0.8 copy-start.16
  564.0 2.8 copy-start.21
  687.2 3.0 copy-start.13
  690.2 1.6 copy-start.12
  691.8 3.5 copy-start.1
  691.9 2.6 copy-start.14
Sparse Core Ops, SparseCore 0:
  11.8 38.3 all-gather.4
  52.0 24.0 all-gather.6
  77.6 37.4 all-gather.8
  116.6 37.4 all-gather.10
  375.0 46.2 reduce-scatter.12
  424.9 36.7 reduce-scatter.6
  464.4 47.8 reduce-scatter.8
  514.8 47.8 reduce-scatter.10
  565.5 121.6 all-reduce.4

commit v2 on v1

--- a/solution.py
+++ b/solution.py
@@ -48,7 +48,7 @@
 
 
 def attend_kernel(
-    heads, head_width, rel_ref, rows_ref, seq_ref, out_ref, probs_ref, skew_ref, keys_ref, values_ref
+    heads, head_width, rel_ref, rows_ref, seq_ref, late_ref, out_ref, probs_ref, skew_ref, keys_ref, values_ref
 ):
     group = heads * head_width
     block = rows_ref.shape[2]
@@ -67,7 +67,7 @@
     def split_heads():
         for head in range(heads):
             keys_ref[head] = head_part(seq_ref, group + head * head_width, head_width)
-            values_ref[head] = head_part(seq_ref, 2 * group + head * head_width, head_width)
+            values_ref[head] = head_part(late_ref, head * head_width, head_width)
 
     mixed = []
     for head in range(heads):
@@ -88,8 +88,8 @@
     out_ref[0, 0] = jnp.concatenate(mixed, axis=-1).astype(jnp.bfloat16)
 
 
-def attend(rel_pad, qkv, heads, head_width):
-    groups, seq_count, piece, triple = qkv.shape
+def attend(rel_pad, pair, late, heads, head_width):
+    groups, seq_count, piece, double = pair.shape
     length = groups * piece
     group = heads * head_width
     pairs = seq_count * heads
@@ -102,8 +102,9 @@
         ),
         in_specs=[
             pl.BlockSpec(rel_pad.shape, lambda s, i: (0, 0)),
-            pl.BlockSpec((1, 1, piece, triple), lambda s, i: (i, s, 0, 0)),
-            pl.BlockSpec((groups, 1, piece, triple), lambda s, i: (0, s, 0, 0)),
+            pl.BlockSpec((1, 1, piece, double), lambda s, i: (i, s, 0, 0)),
+            pl.BlockSpec((groups, 1, piece, double), lambda s, i: (0, s, 0, 0)),
+            pl.BlockSpec((groups, 1, piece, group), lambda s, i: (0, s, 0, 0)),
         ],
         out_specs=(
             pl.BlockSpec((1, 1, piece, group), lambda s, i: (i, s, 0, 0)),
@@ -120,7 +121,7 @@
             bytes_accessed=2 * pairs * length * length,
             transcendentals=pairs * length * length,
         ),
-    )(rel_pad, qkv, qkv)
+    )(rel_pad, pair, pair, late)
 
 
 def attend_back_kernel(
@@ -128,6 +129,7 @@
     head_width,
     rows_ref,
     seq_ref,
+    late_ref,
     grad_ref,
     probs_ref,
     out_ref,
@@ -154,7 +156,7 @@
         value_grad_ref[...] = jnp.zeros_like(value_grad_ref)
         for head in range(heads):
             keys_ref[head] = head_part(seq_ref, group + head * head_width, head_width)
-            values_ref[head] = head_part(seq_ref, 2 * group + head * head_width, head_width)
+            values_ref[head] = head_part(late_ref, head * head_width, head_width)
 
     query_turned = rows_ref[0, 0, :, :group].T
     grad_turned = grad_ref[0, 0].T
@@ -195,8 +197,8 @@
             rel_ref[head : head + 1, :] = folded
 
 
-def attend_back(qkv, grads, probs, heads, head_width):
-    groups, seq_count, piece, triple = qkv.shape
+def attend_back(pair, late, grads, probs, heads, head_width):
+    groups, seq_count, piece, double = pair.shape
     length = groups * piece
     group = heads * head_width
     pairs = seq_count * heads
@@ -204,17 +206,18 @@
         functools.partial(attend_back_kernel, heads, head_width),
         grid=(seq_count, groups),
         out_shape=(
-            jax.ShapeDtypeStruct(qkv.shape, jnp.bfloat16),
+            jax.ShapeDtypeStruct((groups, seq_count, piece, 3 * group), jnp.bfloat16),
             jax.ShapeDtypeStruct((heads, 2 * length), jnp.float32),
         ),
         in_specs=[
-            pl.BlockSpec((1, 1, piece, triple), lambda s, i: (i, s, 0, 0)),
-            pl.BlockSpec((groups, 1, piece, triple), lambda s, i: (0, s, 0, 0)),
+            pl.BlockSpec((1, 1, piece, double), lambda s, i: (i, s, 0, 0)),
+            pl.BlockSpec((groups, 1, piece, double), lambda s, i: (0, s, 0, 0)),
+            pl.BlockSpec((groups, 1, piece, group), lambda s, i: (0, s, 0, 0)),
             pl.BlockSpec((1, 1, piece, group), lambda s, i: (i, s, 0, 0)),
             pl.BlockSpec((1, heads, piece, length), lambda s, i: (s, 0, i, 0)),
         ],
         out_specs=(
-            pl.BlockSpec((groups, 1, piece, triple), lambda s, i: (0, s, 0, 0)),
+            pl.BlockSpec((groups, 1, piece, 3 * group), lambda s, i: (0, s, 0, 0)),
             pl.BlockSpec((heads, 2 * length), lambda s, i: (0, 0)),
         ),
         scratch_shapes=[
@@ -230,7 +233,7 @@
             bytes_accessed=2 * pairs * length * length,
             transcendentals=0,
         ),
-    )(qkv, qkv, grads, probs)
+    )(pair, pair, late, grads, probs)
 
 
 def expert_kernel(
@@ -300,6 +303,24 @@
 
 def exchange(values, axis):
     return lax.all_to_all(values, axis, split_axis=0, concat_axis=0, tiled=True)
+
+
+def halve_over(values, axis):
+    count = lax.axis_size(axis)
+    if count & (count - 1):
+        return lax.psum_scatter(values, axis, scatter_dimension=0, tiled=True)
+    place = lax.axis_index(axis)
+    values = values.reshape(count, values.shape[0] // count, values.shape[1])
+    bit = 1
+    while bit < count:
+        own = (place // bit) % 2
+        halves = values.reshape(values.shape[0] // 2, 2, *values.shape[1:])
+        kept = lax.dynamic_index_in_dim(halves, own, 1, keepdims=False)
+        sent = lax.dynamic_index_in_dim(halves, 1 - own, 1, keepdims=False)
+        arrived = lax.ppermute(sent, axis, [(i, i ^ bit) for i in range(count)])
+        values = (kept.astype(jnp.float32) + arrived.astype(jnp.float32)).astype(jnp.bfloat16)
+        bit *= 2
+    return values[0]
 
 
 def local(
@@ -336,8 +357,9 @@
     def by_group(weight):
         return weight.reshape(shard_rows, groups, group_width).transpose(1, 0, 2)
 
-    projections = jnp.concatenate([by_group(w_query), by_group(w_key), by_group(w_value)], axis=-1)
-    full_qkv = lax.all_gather(projections, ("dp", "expert"), axis=1, tiled=True)
+    projections = jnp.concatenate([by_group(w_query), by_group(w_key)], axis=-1)
+    full_pair = lax.all_gather(projections, ("dp", "expert"), axis=1, tiled=True)
+    full_late = lax.all_gather(by_group(w_value), ("dp", "expert"), axis=1, tiled=True)
     full_output = lax.all_gather(output_projection_weight, ("dp", "expert"), axis=0, tiled=True)
     first_weight = lax.all_gather(expert_in, "dp", axis=1, tiled=True)[0]
     second_weight = lax.all_gather(expert_out, "dp", axis=1, tiled=True)[0]
@@ -346,17 +368,22 @@
     residual_stream = tokens.reshape(rows, width).astype(high)
     normed_one, factor_one = normalize(residual_stream, attn_gain)
     first_layer_norm = normed_one.astype(low)
-    qkv_rows = jnp.einsum(
-        "rm,gmc->grc", first_layer_norm, full_qkv, preferred_element_type=high
-    ).astype(low)
-    qkv = exchange(qkv_rows.reshape(groups, seq_count, piece, triple), "seq")
+
+    def project(weights):
+        projected = jnp.einsum(
+            "rm,gmc->grc", first_layer_norm, weights, preferred_element_type=high
+        ).astype(low)
+        return projected.reshape(groups, seq_count, piece, weights.shape[-1])
+
+    pair = exchange(project(full_pair), "seq")
+    late = exchange(project(full_late), "seq")
 
     head_start = lax.axis_index("seq") * local_heads
     table_part = lax.dynamic_slice_in_dim(bias_table, head_start, local_heads, 1)
     bucket_onehot = (rel_buckets[:, None] == jnp.arange(bucket_count)[None, :]).astype(high)
     bucket_onehot = jnp.pad(bucket_onehot, ((0, 1), (0, 0)))
     rel_pad = jnp.dot(table_part.T, bucket_onehot.T, precision=highest_precision)
-    mixed, probs_kept = attend(rel_pad, qkv, local_heads, head_width)
+    mixed, probs_kept = attend(rel_pad, pair, late, local_heads, head_width)
     attended = exchange(mixed, "seq").reshape(groups, rows, group_width)
     second_branch = residual_stream + jnp.einsum(
         "grc,gcm->rm", attended, output_groups, preferred_element_type=high
@@ -403,44 +430,43 @@
     ).astype(low)
     heads_grad = exchange(attended_grad.reshape(groups, seq_count, piece, group_width), "seq")
     output_weight_grad = jnp.einsum("grc,rm->gcm", attended, grad_low, preferred_element_type=high)
-    qkv_back, rel_back = attend_back(qkv, heads_grad, probs_kept, local_heads, head_width)
+    qkv_back, rel_back = attend_back(pair, late, heads_grad, probs_kept, local_heads, head_width)
     table_local = jnp.dot(bucket_onehot.T, rel_back.T, precision=highest_precision)
     table_grad = lax.dynamic_update_slice_in_dim(
         jnp.zeros((bucket_count, heads_all), high), table_local, head_start, 1
     )
     qkv_tok = exchange(qkv_back, "seq").reshape(groups, rows, triple)
+    first_share = halve_over(first_grad, "dp")
+    second_share = halve_over(second_grad, "dp")
+    output_share = lax.psum_scatter(
+        output_weight_grad.reshape(width, width).astype(low),
+        ("dp", "expert"),
+        scatter_dimension=0,
+        tiled=True,
+    )
+    early_shares = lax.psum((first_share, second_share, output_share), "seq")
+    qkv_tok, early_shares = lax.optimization_barrier((qkv_tok, early_shares))
+    first_share, second_share, output_share = early_shares
     qkv_weight_grad = jnp.einsum(
         "rm,grc->mgc", first_layer_norm, qkv_tok, preferred_element_type=high
     ).astype(low)
-    norm_one_grad = jnp.einsum("grc,gmc->rm", qkv_tok, full_qkv, preferred_element_type=high)
+    norm_one_grad = jnp.einsum(
+        "grc,gmc->rm", qkv_tok[:, :, : 2 * group_width], full_pair, preferred_element_type=high
+    ) + jnp.einsum(
+        "grc,gmc->rm", qkv_tok[:, :, 2 * group_width :], full_late, preferred_element_type=high
+    )
     first_back, attn_gain_grad = norm_back(norm_one_grad, residual_stream, factor_one, attn_gain)
     input_grad = second_grad_total + first_back
 
-    first_share = lax.psum(
-        lax.psum_scatter(first_grad, "dp", scatter_dimension=0, tiled=True), "seq"
-    )
-    second_share = lax.psum(
-        lax.psum_scatter(second_grad, "dp", scatter_dimension=0, tiled=True), "seq"
-    )
-    output_share = lax.psum(
-        lax.psum_scatter(
-            output_weight_grad.reshape(width, width).astype(low),
-            ("dp", "expert"),
-            scatter_dimension=0,
-            tiled=True,
-        ),
-        "seq",
-    )
-    qkv_share = lax.psum(
-        lax.psum_scatter(
-            qkv_weight_grad.reshape(width, groups * triple),
-            ("dp", "expert"),
-            scatter_dimension=0,
-            tiled=True,
-        ),
-        "seq",
-    )
-    qkv_share = qkv_share.astype(high).reshape(shard_rows, groups, triple)
+    qkv_share = lax.psum_scatter(
+        qkv_weight_grad, ("dp", "expert"), scatter_dimension=0, tiled=True
+    )
+    small_totals = lax.psum(
+        (attn_gain_grad, ffn_gain_grad, router_grad, table_grad), ("dp", "expert", "seq")
+    )
+    qkv_share, small_totals = lax.optimization_barrier((qkv_share, small_totals))
+    attn_gain_total, ffn_gain_total, router_total, table_total = small_totals
+    qkv_share = lax.psum(qkv_share, "seq").astype(high)
 
     def from_group(part):
         return (
@@ -448,9 +474,6 @@
             .reshape(shard_rows, width)
         )
 
-    attn_gain_total, ffn_gain_total, router_total, table_total = lax.psum(
-        (attn_gain_grad, ffn_gain_grad, router_grad, table_grad), ("dp", "expert", "seq")
-    )
     return (
         layer_out.reshape(seq_count, piece, width),
         input_grad.reshape(seq_count, piece, width),

time: 703 us -> 594 us (0.84); the launches traced: 702 us -> 584 us
  blocking collectives: 146 us -> 40.1 us
  waiting for transfers between devices: 384 us -> 325 us
  starting transfers between devices: 13.6 us -> 33.9 us
  other arithmetic: 12.4 us -> 23.7 us
  matrix products: 25 us -> 33.8 us
    all_to_all x3 -> x0, blocking collectives: 102 us -> none  [exchange(): return lax.all_to_all(values, axis, split_axis=0, concat_axis=0, tiled=True)]
    reduce_scatter x2 -> x1, waiting for transfers between devices: 101 us -> 0.01 us  [local(): lax.psum_scatter(qkv_weight_grad, ('dp', 'expert'), scatter_dimension=0,...]
    all_to_all x3 -> x7, waiting for transfers between devices: 94.2 us -> 183 us  [exchange(): return lax.all_to_all(values, axis, split_axis=0, concat_axis=0, tiled=True)]
    unnamed x10 -> x9, waiting for transfers between devices: 45.3 us -> 1.86 us
    reduce_scatter x1, waiting for transfers between devices: 38.4 us -> 0.01 us  [local(): lax.psum_scatter(output_weight_grad.reshape(width, width).astype(low), ('...]
    all_to_all x3 -> x7, starting transfers between devices: 13.1 us -> 30.6 us  [exchange(): return lax.all_to_all(values, axis, split_axis=0, concat_axis=0, tiled=True)]
    psum x1 -> x2, waiting for transfers between devices: 69.2 us -> 82.6 us  [the longest x1 48.2 us: local(): early_shares = lax.psum((first_share, second_share, output_share), 'seq')]
    all_gather x1 -> x2, waiting for transfers between devices: 36.5 us -> 47 us  [the longest x1 24.8 us: local(): lax.all_gather(by_group(w_value), ('dp', 'expert'), axis=1, tiled=True)]
  transfers between devices with their start and end apart: 12 -> 20, of which waited for: 9 -> 11; matrix products, arithmetic and copies ran while one was open for 5% -> 14% of each run, Pallas kernels for 3% -> 8%
where the time goes in v2:
time: 594 us; the launch traced here: 584 us
  waiting for transfers between devices  325 us (55%)
  Pallas kernels  73.9 us (12%)
  blocking collectives  40.1 us (7%)
  local copies, waits for them, and re-layouts  38.8 us (7%)
  starting transfers between devices  33.9 us (6%)
  matrix products  33.8 us (6%)
  other arithmetic  23.7 us (4%)
  between operations  14.9 us (3%)
    all_to_all x7, waiting for transfers between devices, exchange(): return lax.all_to_all(values, axis, split_axis=0, concat_axis=0, tiled=True)  183 us
    psum x1, waiting for transfers between devices, local(): early_shares = lax.psum((first_share, second_share, output_share), 'seq')  48.2 us
    psum x1, blocking collectives, local(): lax.psum((attn_gain_grad, ffn_gain_grad, router_grad, table_grad), ('dp',...  40.1 us
    psum x1, waiting for transfers between devices, local(): qkv_share = lax.psum(qkv_share, 'seq').astype(high)  34.4 us
    all_to_all x7, starting transfers between devices, exchange(): return lax.all_to_all(values, axis, split_axis=0, concat_axis=0, tiled=True)  30.6 us
    pallas_call x1, Pallas kernels, attend_back(): pl.pallas_call(functools.partial(attend_back_kernel, heads, head_width),...  26.8 us
    pallas_call x1, Pallas kernels, expert_layer(): pl.pallas_call(functools.partial(expert_kernel, width), grid=(hidden_widt...  25.8 us
    all_gather x1, waiting for transfers between devices, local(): lax.all_gather(by_group(w_value), ('dp', 'expert'), axis=1, tiled=True)  24.8 us
  transfers between devices with their start and end apart: 20, of which 11 were waited for; matrix products, arithmetic and copies ran while one was open for 14% of the time, Pallas kernels for 8%

profile of v2, /device:TPU:0, one launch (start us, length us, event | category | flops | bytes accessed | tf_op | source)
XLA Modules:
  0.0 584.1 jit_solution(7034728434980066449)
XLA Ops:
  7.2 1.8 reshape.182
  9.1 1.1 reshape.179
  10.2 1.1 reshape.180
  11.4 0.8 pad_maximum_fusion
  14.1 24.8 %all-gather.8.cloned.1.call-done = bf16[4,768,192]{2,0,1:T(4,128)(2,1)} async-done(((bf16[4,96,192]{2,0,1:T(4,128)(2,1)}), bf16[4,768,192]{2,0,1:T(4,128)(2,1)}) %all-gather.8.cloned.1.call-update) | async-done | bytes 1179664 | tf_op jit(solution)/shard_map/all_gather | solution.py:362
  38.9 2.7 copy.57
  42.7 0.9 copy.92
  43.6 4.6 all-to-all-start.1
  48.2 22.2 %all-gather.6.cloned.1.call-done = bf16[4,768,384]{2,1,0:T(8,128)(2,1)} async-done(((bf16[4,96,384]{2,1,0:T(8,128)(2,1)}), bf16[4,768,384]{2,1,0:T(8,128)(2,1)}) %all-gather.6.cloned.1.call-update) | async-done | bytes 2359312 | tf_op jit(solution)/shard_map/all_gather | solution.py:361
  70.4 3.3 fusion.19
  73.7 1.6 copy.56
  75.3 4.7 all-to-all-start
  81.0 1.2 fusion.25.rel_ref
  82.2 1.3 copy.59.late_ref
  83.5 33.9 %all-to-all-done.rows_ref.seq_ref = bf16[4,2,256,384]{3,2,1,0:T(8,128)(2,1)S(1)} async-done(((bf16[4,2,256,384]{3,2,1,0:T(8,128)(2,1)}), bf16[4,2,256,384]{3,2,1,0:T(8,128)(2,1)S(1)}, u32[]{:S(2)}, u32[]{:S(2)}) %all-to-all-start) | async-done | bytes 1572896 | tf_op jit(solution)/shard_map/all_to_all | solution.py:305
  117.4 1.1 copy-done.14
  118.6 21.3 %shard_map.229 = (bf16[4,2,256,192]{3,2,1,0:T(8,128)(2,1)}, bf16[2,3,1024,1024]{3,2,1,0:T(8,128)(2,1)}) custom-call(f32[3,2048]{1,0:T(4,128)} %fusion.25.rel_ref, bf16[4,2,256,384]{3,2,1,0:T(8,128)(2,1)} %copy-done.14, bf16[4,2,256,384]{3,2,1,0:T(8,128)(2,1)} %copy-done.14, bf16[4,2,256,192]{3,2,1,0:T(8,128)(2,1)} %copy.59.late_ref), custom_call_target="tpu_custom_call" | custom-call | flops 6442450944 | bytes 12582912 | tf_op jit(solution)/shard_map/pallas_call | solution.py:96
  139.9 2.2 copy.60
  142.1 3.5 all-to-all-start.2
  146.0 19.3 %all-to-all-done.2 = bf16[4,2,256,192]{2,3,1,0:T(8,128)(2,1)S(1)} async-done(((bf16[4,2,256,192]{2,3,1,0:T(8,128)(2,1)}), bf16[4,2,256,192]{2,3,1,0:T(8,128)(2,1)S(1)}, u32[]{:S(2)}, u32[]{:S(2)}) %all-to-all-start.2) | async-done | bytes 786464 | tf_op jit(solution)/shard_map/all_to_all | solution.py:305
  165.4 2.5 multiply_reduce_fusion.2
  169.4 2.6 convolution_convert_fusion
  172.0 4.9 all-to-all-start.3
  177.0 23.0 %all-to-all-done.3 = bf16[2,320,1536]{2,1,0:T(8,128)(2,1)} async-done(((bf16[2,320,1536]{2,1,0:T(8,128)(2,1)}), bf16[2,320,1536]{2,1,0:T(8,128)(2,1)}, u32[]{:S(2)}, u32[]{:S(2)}) %all-to-all-start.3) | async-done | bytes 1966112 | tf_op jit(solution)/shard_map/all_to_all | solution.py:305
  199.9 25.8 %shard_map.230 = (bf16[640,1536]{1,0:T(8,128)(2,1)}, bf16[768,3072]{1,0:T(8,128)(2,1)}, bf16[3072,768]{1,0:T(8,128)(2,1)}) custom-call(bf16[640,1536]{1,0:T(8,128)(2,1)} %bitcast.15.both_ref, bf16[768,3072]{1,0:T(8,128)(2,1)} %bitcast.157, bf16[3072,768]{1,0:T(8,128)(2,1)} %bitcast.158), custom_call_target="tpu_custom_call" | custom-call | flops 18119393280 | bytes 18874368 | tf_op jit(solution)/shard_map/pallas_call | solution.py:273
  225.8 4.8 all-to-all-start.4
  230.6 3.4 dynamic-slice_bitcast_fusion
  233.9 1.6 dynamic-slice_bitcast_fusion.1
  236.0 16.6 %all-to-all-done.4 = bf16[2,320,1536]{2,1,0:T(8,128)(2,1)} async-done(((bf16[2,320,1536]{2,1,0:T(8,128)(2,1)}), bf16[2,320,1536]{2,1,0:T(8,128)(2,1)}, u32[]{:S(2)}, u32[]{:S(2)}) %all-to-all-start.4) | async-done | bytes 1966112 | tf_op jit(solution)/shard_map/all_to_all | solution.py:305
  252.6 3.0 fusion.20
  255.6 1.3 fusion.4
  256.9 1.8 multiply_reduce_fusion
  260.8 1.0 copy.91
  261.7 3.5 all-to-all-start.5
  265.6 1.8 convolution_convert_fusion.3
  267.4 15.6 %all-to-all-done.5 = bf16[4,2,256,192]{2,3,1,0:T(8,128)(2,1)S(1)} async-done(((bf16[4,2,256,192]{2,3,1,0:T(8,128)(2,1)}), bf16[4,2,256,192]{2,3,1,0:T(8,128)(2,1)S(1)}, u32[]{:S(2)}, u32[]{:S(2)}) %all-to-all-start.5) | async-done | bytes 786464 | tf_op jit(solution)/shard_map/all_to_all | solution.py:305
  283.0 1.3 copy.64.grad_ref
  284.3 2.9 fusion
  287.4 1.2 collective-permute-start.3
  288.6 3.5 fusion.1
  292.1 1.2 constant_dynamic-slice_fusion.1
  293.9 0.9 collective-permute-start.1
  294.7 26.8 %shard_map.231 = (bf16[4,2,256,576]{3,2,1,0:T(8,128)(2,1)}, f32[3,2048]{1,0:T(4,128)}) custom-call(bf16[4,2,256,384]{3,2,1,0:T(8,128)(2,1)} %copy-done.14, bf16[4,2,256,384]{3,2,1,0:T(8,128)(2,1)} %copy-done.14, bf16[4,2,256,192]{3,2,1,0:T(8,128)(2,1)} %copy.59.late_ref, bf16[4,2,256,192]{3,2,1,0:T(8,128)(2,1)} %copy.64.grad_ref, ...), custom_call_target="tpu_custom_call" | custom-call | flops 12884901888 | bytes 12582912 | tf_op jit(solution)/shard_map/pallas_call | solution.py:205
  321.5 4.3 copy.65
  325.8 4.5 all-to-all-start.6
  330.4 3.1 fusion.22
  333.5 10.4 %collective-permute-done.1 = bf16[1,192,3072]{2,1,0:T(8,128)(2,1)} collective-permute-done((bf16[1,192,3072]{2,1,0:T(8,128)(2,1)}, bf16[1,192,3072]{2,1,0:T(8,128)(2,1)}, u32[]{:S(2)}, u32[]{:S(2)}) %collective-permute-start.1) | collective-permute-done | bytes 1179680 | tf_op jit(solution)/shard_map/ppermute | solution.py:320
  343.9 2.6 fusion.21
  346.5 74.6 %all-to-all-done.6 = bf16[4,2,256,576]{2,3,1,0:T(8,128)(2,1)} async-done(((bf16[4,2,256,576]{2,3,1,0:T(8,128)(2,1)}), bf16[4,2,256,576]{2,3,1,0:T(8,128)(2,1)}, u32[]{:S(2)}, u32[]{:S(2)}) %all-to-all-start.6) | async-done | bytes 2359328 | tf_op jit(solution)/shard_map/all_to_all | solution.py:305
  421.2 4.4 copy.66
  425.5 48.2 %all-reduce.8.cloned.1.call-done = (bf16[192,3072]{1,0:T(8,128)(2,1)}, bf16[768,768]{1,0:T(8,128)(2,1)}, bf16[96,768]{1,0:T(8,128)(2,1)}) async-done(((bf16[192,3072]{1,0:T(8,128)(2,1)}, bf16[768,768]{1,0:T(8,128)(2,1)}, bf16[96,768]{1,0:T(8,128)(2,1)}), (bf16[192,3072]{1,0:T(8,128)(2,1)}, bf16[768,768]{1,0:T(8,128)(2,1)}, bf16[96,768]{1,0:T(8,128)(2,1)})) %all-reduce.8.cloned.1.call-update) | async-done | bytes 2506768 | tf_op jit(solution)/shard_map/psum | solution.py:447
  473.8 5.9 %convolution_convert_fusion.1 = bf16[768,4,576]{2,0,1:T(8,128)(2,1)} fusion(bf16[4,512,576]{2,1,0:T(8,128)(2,1)} %bitcast.136, bf16[512,768]{1,0:T(8,128)(2,1)S(1)} %copy-done.20), kind=kOutput, calls=%fused_computation.5 | convolution fusion | flops 1813708800 | bytes 6684672 | tf_op jit(solution)/shard_map/rm,grc->mgc/dot_general | solution.py:450
  480.7 1.0 fusion.43
  482.3 4.0 fusion.17
  486.4 4.2 fusion.16
  490.6 40.1 %all-reduce.1 = (f32[768]{0:T(1024)}, f32[768]{0:T(1024)}, f32[768,2]{0,1:T(2,128)}, f32[32,12]{0,1:T(8,128)}) all-reduce(f32[768]{0:T(1024)} %get-tuple-element.46, f32[768]{0:T(1024)} %get-tuple-element.44, f32[768,2]{0,1:T(2,128)} %fusion.43, ...), channel_id=1, replica_groups=mesh['dp'=4,'expert'=2,'seq'=4] {'dp','expert','seq'}, use_global_device_ids=true, to_apply=%region_15.16 | all-reduce | flops 3456 | bytes 27648 | tf_op jit(solution)/shard_map/psum | solution.py:464
  530.6 1.6 bitcast_convert_fusion
  532.3 1.7 bitcast_convert_fusion.1
  534.8 3.0 fusion.13
  537.8 34.4 %all-reduce.6.cloned.1.call-done = bf16[96,4,576]{2,0,1:T(8,128)(2,1)} async-done(((bf16[96,4,576]{2,0,1:T(8,128)(2,1)}), bf16[96,4,576]{2,0,1:T(8,128)(2,1)}) %all-reduce.6.cloned.1.call-update) | async-done | bytes 442384 | tf_op jit(solution)/shard_map/psum | solution.py:469
  572.2 1.3 fusion.45
  573.7 1.0 reshape.194
  575.0 1.0 reshape.195
  576.2 1.0 reshape.196
  (123 shorter events, 12.8 us)
Async XLA Ops:
  7.2 73.8 %copy-start = (f32[32,12]{0,1:T(8,128)S(1)}, f32[32,12]{0,1:T(8,128)}, u32[]{:S(2)}) copy-start(f32[32,12]{0,1:T(8,128)} %param.20) | copy-start | bytes 4612
  7.2 31.7 %all-gather.8.cloned.1.call-start = ((), (), s32[]{:S(2)}) async-start(), calls=%async_computation.10 | async-start | bytes 1769472 | tf_op jit(solution)/shard_map/all_gather | solution.py:362
  9.1 61.4 %all-gather.6.cloned.1.call-start = ((), (), s32[]{:S(2)}) async-start(), calls=%async_computation.9 | async-start | bytes 2654208 | tf_op jit(solution)/shard_map/all_gather | solution.py:361
  11.3 2.3 copy-start.5
  11.4 2.5 copy-start.24
  12.3 153.1 %all-gather.10.cloned.1.call-start = ((), (), s32[]{:S(2)}) async-start(), calls=%async_computation.11 | async-start | bytes 1327104 | tf_op jit(solution)/shard_map/all_gather | solution.py:363
  13.0 163.9 %all-gather.12.cloned.1.call-start = ((), (), s32[]{:S(2)}) async-start(), calls=%async_computation.12 | async-start | bytes 5898240 | tf_op jit(solution)/shard_map/all_gather | solution.py:364
  14.1 28.3 %copy-start.19 = (bf16[512,768]{1,0:T(8,128)(2,1)}, bf16[512,768]{1,0:T(8,128)(2,1)S(1)}, u32[]{:S(2)}) copy-start(bf16[512,768]{1,0:T(8,128)(2,1)S(1)} %fusion.10) | copy-start | bytes 2359300
  41.6 1.0 copy-start.17
  43.6 31.7 %all-to-all-start.1 = ((bf16[4,2,256,192]{2,3,1,0:T(8,128)(2,1)}), bf16[4,2,256,192]{2,3,1,0:T(8,128)(2,1)S(1)}, u32[]{:S(2)}, u32[]{:S(2)}) async-start(bf16[4,2,256,192]{2,3,1,0:T(8,128)(2,1)} %bitcast.126), calls=%async_computation.1 | async-start | bytes 1572864 | tf_op jit(solution)/shard_map/all_to_all | solution.py:305
  75.3 5.3 copy-start.27
  75.3 42.1 %all-to-all-start = ((bf16[4,2,256,384]{3,2,1,0:T(8,128)(2,1)}), bf16[4,2,256,384]{3,2,1,0:T(8,128)(2,1)S(1)}, u32[]{:S(2)}, u32[]{:S(2)}) async-start(bf16[4,2,256,384]{3,2,1,0:T(8,128)(2,1)} %bitcast.5), calls=%async_computation | async-start | bytes 3145728 | tf_op jit(solution)/shard_map/all_to_all | solution.py:305
  80.0 96.9 %all-gather.14.cloned.1.call-start = ((), (), s32[]{:S(2)}) async-start(), calls=%async_computation.13 | async-start | bytes 5898240 | tf_op jit(solution)/shard_map/all_gather | solution.py:365
  117.4 1.1 copy-start.14
  139.9 5.8 copy-start.28
  142.1 23.2 %all-to-all-start.2 = ((bf16[4,2,256,192]{2,3,1,0:T(8,128)(2,1)}), bf16[4,2,256,192]{2,3,1,0:T(8,128)(2,1)S(1)}, u32[]{:S(2)}, u32[]{:S(2)}) async-start(bf16[4,2,256,192]{2,3,1,0:T(8,128)(2,1)} %copy.60), calls=%async_computation.2 | async-start | bytes 1572864 | tf_op jit(solution)/shard_map/all_to_all | solution.py:305
  165.4 2.5 copy-start.12
  165.4 2.5 copy-start.22
  167.9 0.7 copy-start.25
  167.9 1.1 copy-start.9
  168.6 3.4 copy-start.7
  172.0 28.0 %all-to-all-start.3 = ((bf16[2,320,1536]{2,1,0:T(8,128)(2,1)}), bf16[2,320,1536]{2,1,0:T(8,128)(2,1)}, u32[]{:S(2)}, u32[]{:S(2)}) async-start(bf16[2,320,1536]{2,1,0:T(8,128)(2,1)} %bitcast.140), calls=%async_computation.3 | async-start | bytes 3932160 | tf_op jit(solution)/shard_map/all_to_all | solution.py:305
  225.8 26.9 %all-to-all-start.4 = ((bf16[2,320,1536]{2,1,0:T(8,128)(2,1)}), bf16[2,320,1536]{2,1,0:T(8,128)(2,1)}, u32[]{:S(2)}, u32[]{:S(2)}) async-start(bf16[2,320,1536]{2,1,0:T(8,128)(2,1)} %bitcast.139), calls=%async_computation.4 | async-start | bytes 3932160 | tf_op jit(solution)/shard_map/all_to_all | solution.py:305
  230.5 3.4 copy-start.11
  233.9 50.4 %collective-permute-start.2 = (bf16[2,768,768]{2,1,0:T(8,128)(2,1)}, bf16[2,768,768]{2,1,0:T(8,128)(2,1)}, u32[]{:S(2)}, u32[]{:S(2)}) collective-permute-start(bf16[2,768,768]{2,1,0:T(8,128)(2,1)} %dynamic-slice_bitcast_fusion), channel_id=1, source_target_pairs={{0,8},{8,0},{16,24},{24,16},{1,9},{9,1},{17,25},{25,17},{2,10},{10... | collective-permute-start | bytes 7077896 | tf_op jit(solution)/shard_map/ppermute | solution.py:320
  235.5 53.1 %collective-permute-start = (bf16[2,192,3072]{2,1,0:T(8,128)(2,1)}, bf16[2,192,3072]{2,1,0:T(8,128)(2,1)}, u32[]{:S(2)}, u32[]{:S(2)}) collective-permute-start(bf16[2,192,3072]{2,1,0:T(8,128)(2,1)} %dynamic-slice_bitcast_fusion.1), channel_id=1, source_target_pairs={{0,8},{8,0},{16,24},{24,16},{1,9},{9,1},{17,25},{25,17},{2,10},{10... | collective-permute-start | bytes 7077896 | tf_op jit(solution)/shard_map/ppermute | solution.py:320
  256.9 1.8 copy-start.10
  258.7 1.3 copy-start.30
  260.8 4.8 copy-start.13
  261.7 21.3 %all-to-all-start.5 = ((bf16[4,2,256,192]{2,3,1,0:T(8,128)(2,1)}), bf16[4,2,256,192]{2,3,1,0:T(8,128)(2,1)S(1)}, u32[]{:S(2)}, u32[]{:S(2)}) async-start(bf16[4,2,256,192]{2,3,1,0:T(8,128)(2,1)} %bitcast.133), calls=%async_computation.5 | async-start | bytes 1572864 | tf_op jit(solution)/shard_map/all_to_all | solution.py:305
  265.2 81.2 %reduce-scatter.3.cloned.1.call-start = ((), (), s32[]{:S(2)}) async-start(), calls=%async_computation.14 | async-start | bytes 1327104 | tf_op jit(solution)/shard_map/reduce_scatter | solution.py:441
  287.3 4.8 copy-start.2
  287.4 43.0 %collective-permute-start.3 = (bf16[1,768,768]{2,1,0:T(8,128)(2,1)S(1)}, bf16[1,768,768]{2,1,0:T(8,128)(2,1)}, u32[]{:S(2)}, u32[]{:S(2)}) collective-permute-start(bf16[1,768,768]{2,1,0:T(8,128)(2,1)S(1)} %constant_dynamic-slice_fusion), channel_id=1, source_target_pairs={{0,16},{8,24},{16,0},{24,8},{1,17},{9,25},{17,1},{25,9},{2,18},{10... | collective-permute-start | bytes 3538952 | tf_op jit(solution)/shard_map/ppermute | solution.py:320
  292.1 1.8 copy-start.3
  293.9 50.0 %collective-permute-start.1 = (bf16[1,192,3072]{2,1,0:T(8,128)(2,1)}, bf16[1,192,3072]{2,1,0:T(8,128)(2,1)}, u32[]{:S(2)}, u32[]{:S(2)}) collective-permute-start(bf16[1,192,3072]{2,1,0:T(8,128)(2,1)} %constant_dynamic-slice_fusion.1), channel_id=1, source_target_pairs={{0,16},{8,24},{16,0},{24,8},{1,17},{9,25},{17,1},{25,9},{2,18},{10... | collective-permute-start | bytes 3538952 | tf_op jit(solution)/shard_map/ppermute | solution.py:320
  325.8 95.3 %all-to-all-start.6 = ((bf16[4,2,256,576]{2,3,1,0:T(8,128)(2,1)}), bf16[4,2,256,576]{2,3,1,0:T(8,128)(2,1)}, u32[]{:S(2)}, u32[]{:S(2)}) async-start(bf16[4,2,256,576]{2,3,1,0:T(8,128)(2,1)} %copy.65), calls=%async_computation.6 | async-start | bytes 4718592 | tf_op jit(solution)/shard_map/all_to_all | solution.py:305
  330.3 143.4 %all-reduce.8.cloned.1.call-start = ((), (), s32[]{:S(2)}) async-start(), calls=%async_computation.17 | async-start | bytes 5013504 | tf_op jit(solution)/shard_map/psum | solution.py:447
  330.4 13.5 %copy-start.4 = (bf16[2,192,3072]{2,1,0:T(8,128)(2,1)S(1)}, bf16[2,192,3072]{2,1,0:T(8,128)(2,1)}, u32[]{:S(2)}) copy-start(bf16[2,192,3072]{2,1,0:T(8,128)(2,1)} %copy-done.3) | copy-start | bytes 7077892
  346.5 127.3 %copy-start.20 = (bf16[512,768]{1,0:T(8,128)(2,1)S(1)}, bf16[512,768]{1,0:T(8,128)(2,1)}, u32[]{:S(2)}) copy-start(bf16[512,768]{1,0:T(8,128)(2,1)} %copy-done.19) | copy-start | bytes 2359300
  346.5 187.5 %reduce-scatter.5.cloned.1.call-start = ((), (), s32[]{:S(2)}) async-start(), calls=%async_computation.15 | async-start | bytes 4423680 | tf_op jit(solution)/shard_map/reduce_scatter | solution.py:461
  479.6 1.1 copy-start.8
  479.6 2.1 copy-start.23
  479.6 92.6 %all-reduce.6.cloned.1.call-start = ((), (), s32[]{:S(2)}) async-start(), calls=%async_computation.16 | async-start | bytes 983040 | tf_op jit(solution)/shard_map/psum | solution.py:469
  482.3 4.0 copy-start.6
  482.3 4.0 copy-start.18
  486.3 44.3 %copy-start.16 = (bf16[768,768]{1,0:T(8,128)(2,1)S(1)}, bf16[768,768]{1,0:T(8,128)(2,1)}, u32[]{:S(2)}) copy-start(bf16[768,768]{1,0:T(8,128)(2,1)} %get-tuple-element.43) | copy-start | bytes 3538948
  530.6 1.7 copy-start.15
  532.3 1.7 copy-start.29
  532.3 1.7 copy-start.21
  532.3 2.5 copy-start.26
  573.7 3.4 copy-start.1
Sparse Core Ops, SparseCore 0:
  10.5 28.3 all-gather.7
  41.4 29.0 all-gather.5
  72.3 24.0 all-gather.9
  97.8 37.4 all-gather.11
  136.7 37.4 all-gather.13
  269.0 41.7 reduce-scatter.2
  346.6 127.1 all-reduce.7
  479.8 49.4 reduce-scatter.4
  534.1 38.0 all-reduce.5

commit v3 on v1

--- a/solution.py
+++ b/solution.py
@@ -204,7 +204,7 @@
         functools.partial(attend_back_kernel, heads, head_width),
         grid=(seq_count, groups),
         out_shape=(
-            jax.ShapeDtypeStruct(qkv.shape, jnp.bfloat16),
+            jax.ShapeDtypeStruct((groups, seq_count, piece, 3 * group), jnp.bfloat16),
             jax.ShapeDtypeStruct((heads, 2 * length), jnp.float32),
         ),
         in_specs=[
@@ -214,7 +214,7 @@
             pl.BlockSpec((1, heads, piece, length), lambda s, i: (s, 0, i, 0)),
         ],
         out_specs=(
-            pl.BlockSpec((groups, 1, piece, triple), lambda s, i: (0, s, 0, 0)),
+            pl.BlockSpec((groups, 1, piece, 3 * group), lambda s, i: (0, s, 0, 0)),
             pl.BlockSpec((heads, 2 * length), lambda s, i: (0, 0)),
         ),
         scratch_shapes=[
@@ -300,6 +300,24 @@
 
 def exchange(values, axis):
     return lax.all_to_all(values, axis, split_axis=0, concat_axis=0, tiled=True)
+
+
+def halve_over(values, axis):
+    count = lax.axis_size(axis)
+    if count & (count - 1):
+        return lax.psum_scatter(values, axis, scatter_dimension=0, tiled=True)
+    place = lax.axis_index(axis)
+    values = values.reshape(count, values.shape[0] // count, *values.shape[1:])
+    bit = 1
+    while bit < count:
+        own = (place // bit) % 2
+        halves = values.reshape(values.shape[0] // 2, 2, *values.shape[1:])
+        kept = lax.dynamic_index_in_dim(halves, own, 1, keepdims=False)
+        sent = lax.dynamic_index_in_dim(halves, 1 - own, 1, keepdims=False)
+        arrived = lax.ppermute(sent, axis, [(i, i ^ bit) for i in range(count)])
+        values = (kept.astype(jnp.float32) + arrived.astype(jnp.float32)).astype(jnp.bfloat16)
+        bit *= 2
+    return values[0]
 
 
 def local(
@@ -409,6 +427,18 @@
         jnp.zeros((bucket_count, heads_all), high), table_local, head_start, 1
     )
     qkv_tok = exchange(qkv_back, "seq").reshape(groups, rows, triple)
+    first_share = halve_over(first_grad, "dp")
+    second_share = halve_over(second_grad, "dp")
+    output_share = lax.psum_scatter(
+        output_weight_grad.reshape(width, width).astype(low),
+        ("dp", "expert"),
+        scatter_dimension=0,
+        tiled=True,
+    )
+    qkv_tok, shares = lax.optimization_barrier(
+        (qkv_tok, (first_share, second_share, output_share))
+    )
+    early_shares = lax.psum(shares, "seq")
     qkv_weight_grad = jnp.einsum(
         "rm,grc->mgc", first_layer_norm, qkv_tok, preferred_element_type=high
     ).astype(low)
@@ -416,31 +446,16 @@
     first_back, attn_gain_grad = norm_back(norm_one_grad, residual_stream, factor_one, attn_gain)
     input_grad = second_grad_total + first_back
 
-    first_share = lax.psum(
-        lax.psum_scatter(first_grad, "dp", scatter_dimension=0, tiled=True), "seq"
-    )
-    second_share = lax.psum(
-        lax.psum_scatter(second_grad, "dp", scatter_dimension=0, tiled=True), "seq"
-    )
-    output_share = lax.psum(
-        lax.psum_scatter(
-            output_weight_grad.reshape(width, width).astype(low),
-            ("dp", "expert"),
-            scatter_dimension=0,
-            tiled=True,
-        ),
-        "seq",
-    )
-    qkv_share = lax.psum(
-        lax.psum_scatter(
-            qkv_weight_grad.reshape(width, groups * triple),
-            ("dp", "expert"),
-            scatter_dimension=0,
-            tiled=True,
-        ),
-        "seq",
-    )
-    qkv_share = qkv_share.astype(high).reshape(shard_rows, groups, triple)
+    qkv_share = halve_over(halve_over(qkv_weight_grad, "dp"), "expert")
+    qkv_share, small_sums = lax.optimization_barrier(
+        (qkv_share, (attn_gain_grad, ffn_gain_grad, router_grad, table_grad))
+    )
+    attn_gain_total, ffn_gain_total, router_total, table_total = lax.psum(
+        small_sums, ("dp", "expert", "seq")
+    )
+    qkv_share, early_shares = lax.optimization_barrier((qkv_share, early_shares))
+    first_share, second_share, output_share = early_shares
+    qkv_share = lax.psum(qkv_share, "seq").astype(high)
 
     def from_group(part):
         return (
@@ -448,9 +463,6 @@
             .reshape(shard_rows, width)
         )
 
-    attn_gain_total, ffn_gain_total, router_total, table_total = lax.psum(
-        (attn_gain_grad, ffn_gain_grad, router_grad, table_grad), ("dp", "expert", "seq")
-    )
     return (
         layer_out.reshape(seq_count, piece, width),
         input_grad.reshape(seq_count, piece, width),

time: 703 us -> 571 us (0.81); the launches traced: 702 us -> 561 us
  blocking collectives: 146 us -> 40.1 us
  waiting for transfers between devices: 384 us -> 292 us
  other arithmetic: 12.4 us -> 33.6 us
  starting transfers between devices: 13.6 us -> 31.6 us
  local copies, waits for them, and re-layouts: 31.9 us -> 42.4 us
    all_to_all x3 -> x0, blocking collectives: 102 us -> none  [exchange(): return lax.all_to_all(values, axis, split_axis=0, concat_axis=0, tiled=True)]
    reduce_scatter x2 -> x0, waiting for transfers between devices: 101 us -> none  [the longest x1 50.6 us: local(): lax.psum_scatter(first_grad, 'dp', scatter_dimension=0, tiled=True)]
    ppermute x0 -> x7, waiting for transfers between devices: none -> 72.3 us  [halve_over(): arrived = lax.ppermute(sent, axis, [(i, i ^ bit) for i in range(count)])]
    unnamed x10 -> x7, waiting for transfers between devices: 45.3 us -> 1.99 us
    reduce_scatter x1, waiting for transfers between devices: 38.4 us -> 0.01 us  [local(): lax.psum_scatter(output_weight_grad.reshape(width, width).astype(low), ('...]
    all_to_all x3 -> x6, waiting for transfers between devices: 94.2 us -> 126 us  [exchange(): return lax.all_to_all(values, axis, split_axis=0, concat_axis=0, tiled=True)]
    psum x1 -> x2, waiting for transfers between devices: 69.2 us -> 55.2 us  [the longest x1 55.2 us: local(): early_shares = lax.psum(shares, 'seq')]
    all_to_all x3 -> x6, starting transfers between devices: 13.1 us -> 26.3 us  [exchange(): return lax.all_to_all(values, axis, split_axis=0, concat_axis=0, tiled=True)]
  transfers between devices with their start and end apart: 12 -> 20, of which waited for: 9 -> 12; matrix products, arithmetic and copies ran while one was open for 5% -> 13% of each run, Pallas kernels for 3% -> 9%
where the time goes in v3:
time: 571 us; the launch traced here: 561 us
  waiting for transfers between devices  292 us (51%)
  Pallas kernels  73.8 us (13%)
  local copies, waits for them, and re-layouts  42.4 us (7%)
  blocking collectives  40.1 us (7%)
  other arithmetic  33.6 us (6%)
  matrix products  31.7 us (6%)
  starting transfers between devices  31.6 us (6%)
  between operations  15.2 us (3%)
    all_to_all x6, waiting for transfers between devices, exchange(): return lax.all_to_all(values, axis, split_axis=0, concat_axis=0, tiled=True)  126 us
    ppermute x7, waiting for transfers between devices, halve_over(): arrived = lax.ppermute(sent, axis, [(i, i ^ bit) for i in range(count)])  72.3 us
    psum x1, waiting for transfers between devices, local(): early_shares = lax.psum(shares, 'seq')  55.2 us
    psum x1, blocking collectives, local(): lax.psum(small_sums, ('dp', 'expert', 'seq'))  40.1 us
    all_gather x1, waiting for transfers between devices, local(): full_qkv = lax.all_gather(projections, ('dp', 'expert'), axis=1, tiled=True)  36.4 us
    pallas_call x1, Pallas kernels, attend_back(): pl.pallas_call(functools.partial(attend_back_kernel, heads, head_width),...  26.7 us
    all_to_all x6, starting transfers between devices, exchange(): return lax.all_to_all(values, axis, split_axis=0, concat_axis=0, tiled=True)  26.3 us
    pallas_call x1, Pallas kernels, expert_layer(): pl.pallas_call(functools.partial(expert_kernel, width), grid=(hidden_widt...  25.8 us
  transfers between devices with their start and end apart: 20, of which 12 were waited for; matrix products, arithmetic and copies ran while one was open for 13% of the time, Pallas kernels for 9%

profile of v3, /device:TPU:0, one launch (start us, length us, event | category | flops | bytes accessed | tf_op | source)
XLA Modules:
  0.0 561.0 jit_solution(14868210518051414800)
XLA Ops:
  7.2 1.1 reshape.200
  8.4 1.1 reshape.201
  9.5 1.1 reshape.199
  10.7 0.9 pad_maximum_fusion
  13.7 36.4 %all-gather.5.cloned.1.call-done = bf16[4,768,576]{2,1,0:T(8,128)(2,1)} async-done(((bf16[4,96,576]{2,1,0:T(8,128)(2,1)}), bf16[4,768,576]{2,1,0:T(8,128)(2,1)}) %all-gather.5.cloned.1.call-update) | async-done | bytes 3538960 | tf_op jit(solution)/shard_map/all_gather | solution.py:358
  50.1 4.5 convolution_convert_fusion.2
  54.6 1.6 copy.124
  56.2 4.7 all-to-all-start
  62.6 1.2 fusion.23.rel_ref
  63.8 51.4 %all-to-all-done = bf16[4,2,256,576]{2,3,1,0:T(8,128)(2,1)S(1)} async-done(((bf16[4,2,256,576]{2,3,1,0:T(8,128)(2,1)}), bf16[4,2,256,576]{2,3,1,0:T(8,128)(2,1)S(1)}, u32[]{:S(2)}, u32[]{:S(2)}) %all-to-all-start) | async-done | bytes 2359328 | tf_op jit(solution)/shard_map/all_to_all | solution.py:302
  115.2 2.6 copy.91.rows_ref.seq_ref
  117.7 21.3 %shard_map.229 = (bf16[4,2,256,192]{3,2,1,0:T(8,128)(2,1)}, bf16[2,3,1024,1024]{3,2,1,0:T(8,128)(2,1)}) custom-call(f32[3,2048]{1,0:T(4,128)} %fusion.23.rel_ref, bf16[4,2,256,576]{3,2,1,0:T(8,128)(2,1)} %copy.91.rows_ref.seq_ref, bf16[4,2,256,576]{3,2,1,0:T(8,128)(2,1)} %copy.91.rows_ref.seq_ref), custom_call_target="tpu_custom_call" | custom-call | flops 6442450944 | bytes 12582912 | tf_op jit(solution)/shard_map/pallas_call | solution.py:96
  139.0 2.2 copy.93
  141.2 3.6 all-to-all-start.1
  145.2 19.3 %all-to-all-done.1 = bf16[4,2,256,192]{2,3,1,0:T(8,128)(2,1)S(1)} async-done(((bf16[4,2,256,192]{2,3,1,0:T(8,128)(2,1)}), bf16[4,2,256,192]{2,3,1,0:T(8,128)(2,1)S(1)}, u32[]{:S(2)}, u32[]{:S(2)}) %all-to-all-start.1) | async-done | bytes 786464 | tf_op jit(solution)/shard_map/all_to_all | solution.py:302
  164.6 2.5 multiply_reduce_fusion.2
  168.6 2.6 convolution_convert_fusion
  171.1 4.9 all-to-all-start.2
  176.1 22.9 %all-to-all-done.2 = bf16[2,320,1536]{2,1,0:T(8,128)(2,1)} async-done(((bf16[2,320,1536]{2,1,0:T(8,128)(2,1)}), bf16[2,320,1536]{2,1,0:T(8,128)(2,1)}, u32[]{:S(2)}, u32[]{:S(2)}) %all-to-all-start.2) | async-done | bytes 1966112 | tf_op jit(solution)/shard_map/all_to_all | solution.py:302
  199.1 25.8 %shard_map.230 = (bf16[640,1536]{1,0:T(8,128)(2,1)}, bf16[768,3072]{1,0:T(8,128)(2,1)}, bf16[3072,768]{1,0:T(8,128)(2,1)}) custom-call(bf16[640,1536]{1,0:T(8,128)(2,1)} %bitcast.10.both_ref, bf16[768,3072]{1,0:T(8,128)(2,1)} %bitcast.170, bf16[3072,768]{1,0:T(8,128)(2,1)} %bitcast.171), custom_call_target="tpu_custom_call" | custom-call | flops 18119393280 | bytes 18874368 | tf_op jit(solution)/shard_map/pallas_call | solution.py:270
  224.9 4.8 all-to-all-start.3
  229.7 22.1 %all-to-all-done.3 = bf16[2,320,1536]{2,1,0:T(8,128)(2,1)} async-done(((bf16[2,320,1536]{2,1,0:T(8,128)(2,1)}), bf16[2,320,1536]{2,1,0:T(8,128)(2,1)}, u32[]{:S(2)}, u32[]{:S(2)}) %all-to-all-start.3) | async-done | bytes 1966112 | tf_op jit(solution)/shard_map/all_to_all | solution.py:302
  251.8 3.0 fusion.18
  254.7 1.3 fusion.5
  256.0 1.8 multiply_reduce_fusion
  260.8 3.7 all-to-all-start.4
  264.5 3.2 dynamic-slice_bitcast_fusion
  267.8 3.2 dynamic-slice_bitcast_fusion.1
  271.5 10.7 %all-to-all-done.4 = bf16[4,2,256,192]{2,3,1,0:T(8,128)(2,1)S(1)} async-done(((bf16[4,2,256,192]{2,3,1,0:T(8,128)(2,1)}), bf16[4,2,256,192]{2,3,1,0:T(8,128)(2,1)S(1)}, u32[]{:S(2)}, u32[]{:S(2)}) %all-to-all-start.4) | async-done | bytes 786464 | tf_op jit(solution)/shard_map/all_to_all | solution.py:302
  282.2 1.3 copy.98.grad_ref
  283.5 26.7 %shard_map.231 = (bf16[4,2,256,576]{3,2,1,0:T(8,128)(2,1)}, f32[3,2048]{1,0:T(4,128)}) custom-call(bf16[4,2,256,576]{3,2,1,0:T(8,128)(2,1)} %copy.91.rows_ref.seq_ref, bf16[4,2,256,576]{3,2,1,0:T(8,128)(2,1)} %copy.91.rows_ref.seq_ref, bf16[4,2,256,192]{3,2,1,0:T(8,128)(2,1)} %copy.98.grad_ref, bf16[2,3,1024,1024]{3,2,1,0:T(8,128)(2,1)} %get-tuple-element.34.probs_ref), custom_call_target="tpu_custom_call" | custom-call | flops 12884901888 | bytes 12582912 | tf_op jit(solution)/shard_map/pallas_call | solution.py:203
  310.2 4.3 copy.99
  314.6 4.5 all-to-all-start.5
  319.1 2.9 fusion
  322.2 1.4 collective-permute-start.3
  323.6 3.3 fusion.1
  326.9 1.1 constant_dynamic-slice_fusion.3
  329.4 1.8 convolution_convert_fusion.3
  331.3 20.0 %collective-permute-done.3 = bf16[1,768,768]{2,1,0:T(8,128)(2,1)} collective-permute-done((bf16[1,768,768]{2,1,0:T(8,128)(2,1)S(1)}, bf16[1,768,768]{2,1,0:T(8,128)(2,1)}, u32[]{:S(2)}, u32[]{:S(2)}) %collective-permute-start.3) | collective-permute-done | bytes 1179680 | tf_op jit(solution)/shard_map/ppermute | solution.py:317
  351.3 3.1 fusion.20
  354.3 24.3 %collective-permute-done.1 = bf16[1,192,3072]{2,1,0:T(8,128)(2,1)} collective-permute-done((bf16[1,192,3072]{2,1,0:T(8,128)(2,1)}, bf16[1,192,3072]{2,1,0:T(8,128)(2,1)}, u32[]{:S(2)}, u32[]{:S(2)}) %collective-permute-start.1) | collective-permute-done | bytes 1179680 | tf_op jit(solution)/shard_map/ppermute | solution.py:317
  378.6 2.6 fusion.19
  381.2 3.3 copy.114
  384.6 5.4 convolution_convert_fusion.1
  390.0 5.9 %copy.103 = bf16[768,4,576]{2,0,1:T(8,128)(2,1)} copy(bf16[768,4,576]{0,2,1:T(8,128)(2,1)} %convolution_convert_fusion.1) | data formatting | bytes 7077888 | tf_op jit(solution)/shard_map/convert_element_type | solution.py:444
  395.9 4.5 constant_dynamic-slice_fusion.1
  401.6 3.2 collective-permute-done.4
  404.7 3.3 fusion.2
  408.1 1.0 constant_dynamic-slice_fusion
  409.1 1.3 collective-permute-start.5
  410.4 1.0 fusion.42
  412.0 6.2 %fusion.10 = (f32[768]{0:T(1024)}, f32[512]{0:T(512)S(1)}, f32[512,768,1]{1,0,2:T(8,128)S(1)}) fusion(bf16[2,256,768]{2,1,0:T(8,128)(2,1)} %param.14, f32[512]{0:T(512)S(1)} %bitcast.167, f32[768]{0:T(1024)} %param.15, bf16[4,512,576]{1,2,0:T(8,128)(2,1)} %bitcast.151, bf16[4,768,576]{2,1,0:T(8,128)(2,1)} %all-gather.5.cloned.1.call-done), kind=kOutput, calls=%fused_computation.30 | convolution fusion | flops 1814690560 | bytes 8267776 | tf_op jit(solution)/shard_map/grc,gmc->rm/dot_general | solution.py:445
  418.1 15.0 %collective-permute-done.5 = bf16[1,192,4,576]{3,1,2,0:T(8,128)(2,1)} collective-permute-done((bf16[1,192,4,576]{3,1,2,0:T(8,128)(2,1)}, bf16[1,192,4,576]{3,1,2,0:T(8,128)(2,1)}, u32[]{:S(2)}, u32[]{:S(2)}) %collective-permute-start.5) | collective-permute-done | bytes 884768 | tf_op jit(solution)/shard_map/ppermute | solution.py:317
  433.1 1.5 add_convert_fusion.2
  435.6 1.6 fusion.16
  437.2 9.9 %collective-permute-done.6 = bf16[1,96,4,576]{3,1,2,0:T(8,128)(2,1)S(1)} collective-permute-done((bf16[1,96,4,576]{3,1,2,0:T(8,128)(2,1)S(1)}, bf16[1,96,4,576]{3,1,2,0:T(8,128)(2,1)S(1)}, u32[]{:S(2)}, u32[]{:S(2)}) %collective-permute-start.6) | collective-permute-done | bytes 442400 | tf_op jit(solution)/shard_map/ppermute | solution.py:317
  448.0 55.2 %all-reduce.8.cloned.1.call-done = (bf16[192,3072]{1,0:T(8,128)(2,1)}, bf16[768,768]{1,0:T(8,128)(2,1)}, bf16[96,768]{1,0:T(8,128)(2,1)}) async-done(((bf16[192,3072]{1,0:T(8,128)(2,1)}, bf16[768,768]{1,0:T(8,128)(2,1)}, bf16[96,768]{1,0:T(8,128)(2,1)}), (bf16[192,3072]{1,0:T(8,128)(2,1)}, bf16[768,768]{1,0:T(8,128)(2,1)}, bf16[96,768]{1,0:T(8,128)(2,1)})) %all-reduce.8.cloned.1.call-update) | async-done | bytes 2506768 | tf_op jit(solution)/shard_map/psum | solution.py:441
  503.2 3.0 bitcast_convert_fusion.1
  507.0 40.1 %all-reduce.1 = (f32[768]{0:T(1024)}, f32[32,12]{0,1:T(8,128)}, f32[768]{0:T(1024)}, f32[768,2]{0,1:T(2,128)}) all-reduce(f32[768]{0:T(1024)S(1)} %copy-done.31, f32[32,12]{0,1:T(8,128)S(1)} %dynamic_update_slice.3, f32[768]{0:T(1024)S(1)} %copy-done.27, ...), channel_id=1, replica_groups=mesh['dp'=4,'expert'=2,'seq'=4] {'dp','expert','seq'}, use_global_device_ids=true, to_apply=%region_12.13 | all-reduce | flops 3456 | bytes 27648 | tf_op jit(solution)/shard_map/psum | solution.py:453
  547.2 1.6 bitcast_convert_fusion
  548.7 1.3 fusion.44
  550.3 1.0 reshape.213
  551.5 1.0 reshape.214
  552.7 1.0 reshape.215
  (131 shorter events, 15.7 us)
Async XLA Ops:
  7.2 55.4 %copy-start = (f32[32,12]{0,1:T(8,128)S(1)}, f32[32,12]{0,1:T(8,128)}, u32[]{:S(2)}) copy-start(f32[32,12]{0,1:T(8,128)} %param.20) | copy-start | bytes 4612
  7.2 42.9 %all-gather.5.cloned.1.call-start = ((), (), s32[]{:S(2)}) async-start(), calls=%async_computation.7 | async-start | bytes 4423680 | tf_op jit(solution)/shard_map/all_gather | solution.py:358
  10.7 2.5 copy-start.5
  11.6 1.8 copy-start.25
  11.6 153.0 %all-gather.7.cloned.1.call-start = ((), (), s32[]{:S(2)}) async-start(), calls=%async_computation.8 | async-start | bytes 1327104 | tf_op jit(solution)/shard_map/all_gather | solution.py:359
  12.4 163.7 %all-gather.9.cloned.1.call-start = ((), (), s32[]{:S(2)}) async-start(), calls=%async_computation.9 | async-start | bytes 5898240 | tf_op jit(solution)/shard_map/all_gather | solution.py:360
  13.7 41.0 %copy-start.17 = (bf16[512,768]{1,0:T(8,128)(2,1)}, bf16[512,768]{1,0:T(8,128)(2,1)S(1)}, u32[]{:S(2)}) copy-start(bf16[512,768]{1,0:T(8,128)(2,1)S(1)} %fusion.13) | copy-start | bytes 2359300
  56.2 5.3 copy-start.30
  56.2 59.0 %all-to-all-start = ((bf16[4,2,256,576]{2,3,1,0:T(8,128)(2,1)}), bf16[4,2,256,576]{2,3,1,0:T(8,128)(2,1)S(1)}, u32[]{:S(2)}, u32[]{:S(2)}) async-start(bf16[4,2,256,576]{2,3,1,0:T(8,128)(2,1)} %bitcast.140), calls=%async_computation | async-start | bytes 4718592 | tf_op jit(solution)/shard_map/all_to_all | solution.py:302
  61.0 115.2 %all-gather.11.cloned.1.call-start = ((), (), s32[]{:S(2)}) async-start(), calls=%async_computation.10 | async-start | bytes 5898240 | tf_op jit(solution)/shard_map/all_gather | solution.py:361
  61.9 0.7 copy-start.14
  139.0 5.9 %copy-start.32 = (s32[2,256]{1,0:T(2,128)S(1)}, s32[2,256]{1,0:T(2,128)}, u32[]{:S(2)}) copy-start(s32[2,256]{1,0:T(2,128)} %param.26) | copy-start | bytes 6148
  141.2 23.4 %copy-start.6 = (bf16[2,256,768]{2,1,0:T(8,128)(2,1)S(1)}, bf16[2,256,768]{2,1,0:T(8,128)(2,1)}, u32[]{:S(2)}) copy-start(bf16[2,256,768]{2,1,0:T(8,128)(2,1)} %param.14) | copy-start | bytes 2359300
  141.2 23.3 %all-to-all-start.1 = ((bf16[4,2,256,192]{2,3,1,0:T(8,128)(2,1)}), bf16[4,2,256,192]{2,3,1,0:T(8,128)(2,1)S(1)}, u32[]{:S(2)}, u32[]{:S(2)}) async-start(bf16[4,2,256,192]{2,3,1,0:T(8,128)(2,1)} %copy.93), calls=%async_computation.1 | async-start | bytes 1572864 | tf_op jit(solution)/shard_map/all_to_all | solution.py:302
  164.6 2.5 copy-start.12
  164.6 2.5 copy-start.20
  167.1 0.7 copy-start.28
  167.1 1.1 copy-start.10
  167.8 3.4 copy-start.8
  171.1 27.9 %all-to-all-start.2 = ((bf16[2,320,1536]{2,1,0:T(8,128)(2,1)}), bf16[2,320,1536]{2,1,0:T(8,128)(2,1)}, u32[]{:S(2)}, u32[]{:S(2)}) async-start(bf16[2,320,1536]{2,1,0:T(8,128)(2,1)} %bitcast.155), calls=%async_computation.2 | async-start | bytes 3932160 | tf_op jit(solution)/shard_map/all_to_all | solution.py:302
  224.9 26.9 %all-to-all-start.3 = ((bf16[2,320,1536]{2,1,0:T(8,128)(2,1)}), bf16[2,320,1536]{2,1,0:T(8,128)(2,1)}, u32[]{:S(2)}, u32[]{:S(2)}) async-start(bf16[2,320,1536]{2,1,0:T(8,128)(2,1)} %bitcast.154), calls=%async_computation.3 | async-start | bytes 3932160 | tf_op jit(solution)/shard_map/all_to_all | solution.py:302
  256.0 1.8 copy-start.23
  256.0 1.8 copy-start.11
  257.8 1.3 copy-start.33
  260.8 21.4 %all-to-all-start.4 = ((bf16[4,2,256,192]{2,3,1,0:T(8,128)(2,1)}), bf16[4,2,256,192]{2,3,1,0:T(8,128)(2,1)S(1)}, u32[]{:S(2)}, u32[]{:S(2)}) async-start(bf16[4,2,256,192]{2,3,1,0:T(8,128)(2,1)} %bitcast.137), calls=%async_computation.4 | async-start | bytes 1572864 | tf_op jit(solution)/shard_map/all_to_all | solution.py:302
  267.8 51.4 %collective-permute-start.2 = (bf16[2,768,768]{2,1,0:T(8,128)(2,1)}, bf16[2,768,768]{2,1,0:T(8,128)(2,1)}, u32[]{:S(2)}, u32[]{:S(2)}) collective-permute-start(bf16[2,768,768]{2,1,0:T(8,128)(2,1)} %dynamic-slice_bitcast_fusion), channel_id=1, source_target_pairs={{0,8},{8,0},{16,24},{24,16},{1,9},{9,1},{17,25},{25,17},{2,10},{10... | collective-permute-start | bytes 7077896 | tf_op jit(solution)/shard_map/ppermute | solution.py:317
  271.0 52.6 %collective-permute-start = (bf16[2,192,3072]{2,1,0:T(8,128)(2,1)}, bf16[2,192,3072]{2,1,0:T(8,128)(2,1)}, u32[]{:S(2)}, u32[]{:S(2)}) collective-permute-start(bf16[2,192,3072]{2,1,0:T(8,128)(2,1)} %dynamic-slice_bitcast_fusion.1), channel_id=1, source_target_pairs={{0,8},{8,0},{16,24},{24,16},{1,9},{9,1},{17,25},{25,17},{2,10},{10... | collective-permute-start | bytes 7077896 | tf_op jit(solution)/shard_map/ppermute | solution.py:317
  314.6 66.7 %all-to-all-start.5 = ((bf16[4,2,256,576]{2,3,1,0:T(8,128)(2,1)}), bf16[4,2,256,576]{2,3,1,0:T(8,128)(2,1)}, u32[]{:S(2)}, u32[]{:S(2)}) async-start(bf16[4,2,256,576]{2,3,1,0:T(8,128)(2,1)} %copy.99), calls=%async_computation.5 | async-start | bytes 4718592 | tf_op jit(solution)/shard_map/all_to_all | solution.py:302
  319.1 65.5 %reduce-scatter.2.cloned.1.call-start = ((), (), s32[]{:S(2)}) async-start(), calls=%async_computation.11 | async-start | bytes 1327104 | tf_op jit(solution)/shard_map/reduce_scatter | solution.py:432
  322.1 4.8 copy-start.2
  322.2 29.1 %collective-permute-start.3 = (bf16[1,768,768]{2,1,0:T(8,128)(2,1)S(1)}, bf16[1,768,768]{2,1,0:T(8,128)(2,1)}, u32[]{:S(2)}, u32[]{:S(2)}) collective-permute-start(bf16[1,768,768]{2,1,0:T(8,128)(2,1)S(1)} %constant_dynamic-slice_fusion.2), channel_id=1, source_target_pairs={{0,16},{8,24},{16,0},{24,8},{1,17},{9,25},{17,1},{25,9},{2,18},{10... | collective-permute-start | bytes 3538952 | tf_op jit(solution)/shard_map/ppermute | solution.py:317
  326.9 1.8 copy-start.3
  326.9 2.4 copy-start.13
  328.7 49.9 %collective-permute-start.1 = (bf16[1,192,3072]{2,1,0:T(8,128)(2,1)}, bf16[1,192,3072]{2,1,0:T(8,128)(2,1)}, u32[]{:S(2)}, u32[]{:S(2)}) collective-permute-start(bf16[1,192,3072]{2,1,0:T(8,128)(2,1)} %constant_dynamic-slice_fusion.3), channel_id=1, source_target_pairs={{0,16},{8,24},{16,0},{24,8},{1,17},{9,25},{17,1},{25,9},{2,18},{10... | collective-permute-start | bytes 3538952 | tf_op jit(solution)/shard_map/ppermute | solution.py:317
  331.2 172.0 %all-reduce.8.cloned.1.call-start = ((), (), s32[]{:S(2)}) async-start(), calls=%async_computation.13 | async-start | bytes 5013504 | tf_op jit(solution)/shard_map/psum | solution.py:441
  331.2 47.4 %copy-start.4 = (bf16[2,192,3072]{2,1,0:T(8,128)(2,1)S(1)}, bf16[2,192,3072]{2,1,0:T(8,128)(2,1)}, u32[]{:S(2)}) copy-start(bf16[2,192,3072]{2,1,0:T(8,128)(2,1)} %copy-done.3) | copy-start | bytes 7077892
  381.2 3.3 copy-start.18
  400.6 4.2 collective-permute-start.4
  401.3 147.4 %all-reduce.6.cloned.1.call-start = ((), (), s32[]{:S(2)}) async-start(), calls=%async_computation.12 | async-start | bytes 983040 | tf_op jit(solution)/shard_map/psum | solution.py:458
  408.0 2.4 copy-start.9
  408.0 2.4 copy-start.24
  408.1 3.4 copy-start.15
  408.1 3.4 copy-start.21
  409.1 24.0 %collective-permute-start.5 = (bf16[1,192,4,576]{3,1,2,0:T(8,128)(2,1)}, bf16[1,192,4,576]{3,1,2,0:T(8,128)(2,1)}, u32[]{:S(2)}, u32[]{:S(2)}) collective-permute-start(bf16[1,192,4,576]{3,1,2,0:T(8,128)(2,1)} %constant_dynamic-slice_fusion), channel_id=1, source_target_pairs={{0,16},{8,24},{16,0},{24,8},{1,17},{9,25},{17,1},{25,9},{2,18},{10... | collective-permute-start | bytes 2654216 | tf_op jit(solution)/shard_map/ppermute | solution.py:317
  418.1 17.5 %copy-start.7 = (bf16[2,256,768]{2,1,0:T(8,128)(2,1)S(1)}, bf16[2,256,768]{2,1,0:T(8,128)(2,1)}, u32[]{:S(2)}) copy-start(bf16[2,256,768]{2,1,0:T(8,128)(2,1)} %param.14) | copy-start | bytes 2359300
  418.1 17.5 %copy-start.26 = (f32[768]{0:T(1024)S(1)}, f32[768]{0:T(1024)}, u32[]{:S(2)}) copy-start(f32[768]{0:T(1024)} %param.15) | copy-start | bytes 9220
  418.1 17.5 %copy-start.29 = (f32[512]{0:T(512)S(1)}, f32[512]{0:T(512)}, u32[]{:S(2)}) copy-start(f32[512]{0:T(512)} %multiply_multiply_fusion) | copy-start | bytes 6148
  434.7 12.4 %collective-permute-start.6 = (bf16[1,96,4,576]{3,1,2,0:T(8,128)(2,1)S(1)}, bf16[1,96,4,576]{3,1,2,0:T(8,128)(2,1)S(1)}, u32[]{:S(2)}, u32[]{:S(2)}) collective-permute-start(bf16[1,96,4,576]{3,1,2,0:T(8,128)(2,1)S(1)} %dynamic-slice_bitcast_fusion.2), channel_id=1, source_target_pairs={{0,4},{4,0},{1,5},{5,1},{2,6},{6,2},{3,7},{7,3},{8,12},{12,8},{9,1... | collective-permute-start | bytes 1327112 | tf_op jit(solution)/shard_map/ppermute | solution.py:317
  503.2 3.1 copy-start.19
  503.2 3.8 copy-start.22
  503.2 3.8 copy-start.27
  503.2 3.8 copy-start.31
  503.2 43.9 %copy-start.16 = (bf16[768,768]{1,0:T(8,128)(2,1)S(1)}, bf16[768,768]{1,0:T(8,128)(2,1)}, u32[]{:S(2)}) copy-start(bf16[768,768]{1,0:T(8,128)(2,1)} %get-tuple-element.51) | copy-start | bytes 3538948
  550.3 3.4 copy-start.1
Sparse Core Ops, SparseCore 0:
  11.8 38.3 all-gather.4
  52.0 24.0 all-gather.6
  77.6 37.4 all-gather.8
  116.6 37.4 all-gather.10
  331.3 41.8 reduce-scatter.1
  401.4 101.6 all-reduce.7
  505.5 37.1 all-reduce.5
